TPU v7x, 256 devices: a whole 4x4x8 slice. The times are simulated.
256 devices in a mesh: dp: 128 (over y, x, z), rep: 2 (over core).
Axes of the slice: x: 4, y: 4, z: 8, core: 2. Of those that a mesh axis runs over, the one named last changes fastest.
Arguments:
- embeddings: bfloat16 [32768, 1024], P(('dp', 'rep')), may hold values from -15 to 15
- parents: int32 [32768], P(('dp', 'rep')), may hold values from 0 to 63, as said below
- block_lists: int32 [64, 16], replicated, may hold values from 0 to 1023, as said below
- centroids: bfloat16 [262144, 1024], P('dp'), may hold values from -6.5 to 6.5
Outputs:
- new_centroids: float32 [262144, 1024], P('dp', 'rep')
- spread: float32 [32768], P(('dp', 'rep'))
Inputs may be any that keep to these rules, and one draw needn't show every extreme that they name: `parents`: among the 128 embeddings of one device at most 4 share a parent, and on every device some parent has exactly 4. `block_lists`: each of the 1024 blocks stands in exactly one parent's list.
All inputs are finite; a program needn't handle non-finite values.
Results may differ from a plain program's by a relative error of at most 0.0017.
Values may be sent and summed in bfloat16 or wider, within the bound.
A program may use at most 128 MiB of HBM per device.

v0:
```python
import math

import jax
import jax.numpy as jnp
from jax import lax
from jax.sharding import PartitionSpec as P

BETA = 3.0
LAMBDA = 0.25
EMPTY_NORM = 1e30


def score_blocks(incoming, served, scale):
    return jnp.einsum("kmd,kjd->kmj", incoming, served, preferred_element_type=jnp.float32) * scale


def local(embeddings, parents, block_lists, centroids):
    rows_dev, width = embeddings.shape
    parent_count, list_len = block_lists.shape
    total_blocks = parent_count * list_len
    dp_size = lax.axis_size("dp")
    rep_size = lax.axis_size("rep")
    own_blocks = total_blocks // dp_size
    block_rows = centroids.shape[0] // own_blocks
    capacity = 2 * rows_dev * list_len // total_blocks
    scale = BETA / math.sqrt(width)
    member = (parents[:, None] == jnp.arange(parent_count, dtype=jnp.int32)[None, :]).astype(
        jnp.int32
    )
    running = jnp.cumsum(member, axis=0)
    ranking = jnp.sum(member * (running - 1), axis=1)
    counts = running[-1]
    slot_of = parents * capacity + ranking
    picker = (
        slot_of[None, :] == jnp.arange(parent_count * capacity, dtype=jnp.int32)[:, None]
    ).astype(jnp.bfloat16)
    packed = jnp.dot(picker, embeddings, preferred_element_type=jnp.float32).astype(jnp.bfloat16)
    location = jnp.argsort(block_lists.reshape(-1))
    send_index = (location // list_len)[:, None] * capacity + jnp.arange(capacity, dtype=jnp.int32)[
        None, :
    ]
    local_blocks = centroids.reshape(own_blocks, block_rows, width)
    send_order = jnp.transpose(send_index.reshape(dp_size, own_blocks, capacity), (1, 0, 2))
    outgoing = packed[send_order]
    incoming = lax.all_to_all(outgoing, "dp", split_axis=1, concat_axis=1, tiled=True).reshape(
        own_blocks, dp_size * capacity, width
    )
    scores = score_blocks(incoming, local_blocks, scale)
    block_max = jnp.max(scores, axis=2)
    block_sum = jnp.sum(jnp.exp(scores - block_max[..., None]), axis=2)
    returned_max, returned_sum = (
        lax.all_to_all(
            block_max.reshape(own_blocks, dp_size, capacity),
            "dp",
            split_axis=1,
            concat_axis=1,
            tiled=True,
        ),
        lax.all_to_all(
            block_sum.reshape(own_blocks, dp_size, capacity),
            "dp",
            split_axis=1,
            concat_axis=1,
            tiled=True,
        ),
    )
    returned_max = jnp.transpose(returned_max, (1, 0, 2))
    returned_sum = jnp.transpose(returned_sum, (1, 0, 2))
    gathered_max = returned_max.reshape(total_blocks, capacity)[block_lists]
    gathered_sum = returned_sum.reshape(total_blocks, capacity)[block_lists]
    highest = jnp.max(gathered_max, axis=1)
    summed = jnp.sum(gathered_sum * jnp.exp(gathered_max - highest[:, None, :]), axis=1)
    filled = jnp.arange(capacity, dtype=jnp.int32)[None, :] < counts[:, None]
    lognorm = jnp.where(filled, highest + jnp.log(summed), EMPTY_NORM)
    spread = jnp.log(summed).reshape(-1)[slot_of]
    norm_blocks = lognorm.reshape(-1)[send_order]
    lognorms = lax.all_to_all(norm_blocks, "dp", split_axis=1, concat_axis=1, tiled=True).reshape(
        own_blocks, dp_size * capacity
    )
    scores = score_blocks(incoming, local_blocks, scale)
    responsibility = jnp.exp(scores - lognorms[..., None])
    masses = jnp.sum(responsibility, axis=1)
    weights = responsibility.astype(jnp.bfloat16)
    sum_rows = jnp.einsum("kmj,kmd->kjd", weights, incoming, preferred_element_type=jnp.float32)
    mass_wide = jnp.broadcast_to(masses[..., None], masses.shape + (rep_size,))
    piece = width // rep_size
    combined, mass_total = (
        lax.psum_scatter(sum_rows, "rep", scatter_dimension=2, tiled=True),
        lax.psum_scatter(mass_wide, "rep", scatter_dimension=2, tiled=True),
    )
    previous = lax.dynamic_slice_in_dim(
        local_blocks, lax.axis_index("rep") * piece, piece, 2
    ).astype(jnp.float32)
    fresh = (combined + LAMBDA * previous) / (mass_total + LAMBDA)
    return (fresh.reshape(own_blocks * block_rows, piece), spread)


def solution(mesh):
    placed = (P(("dp", "rep"), None), P(("dp", "rep")), P(), P("dp", None))
    return jax.shard_map(
        local,
        mesh=mesh,
        in_specs=placed,
        out_specs=(P("dp", "rep"), P(("dp", "rep"))),
        check_vma=False,
    )
```

profile of v0, /device:TPU:1, one launch (start us, length us, event | category | flops | bytes accessed | tf_op | source)
XLA Modules:
  0.0 435.0 jit_solution(2810153479252120580)
XLA Ops:
  7.2 0.0 copy-start
  7.2 0.8 copy.16
  8.0 0.1 reshape.69
  8.1 4.4 %sort.17 = (s32[1024]{0:T(1024)}, s32[1024]{0:T(1024)S(1)}) sort(s32[1024]{0:T(1024)S(1)} %reshape.69, s32[1024]{0:T(1024)S(1)} %iota.23), dimensions={0}, to_apply=%region_2.3 | sort | flops 10240 | bytes 16384 | tf_op jit(solution)/shard_map/jit(argsort)/sort | solution.py:38
  12.5 0.1 add.69
  12.6 0.8 fusion.10
  13.4 0.2 reduce_window_sum.11
  13.5 0.8 select_reduce_fusion
  14.4 1.2 compare_select_fusion.2
  15.6 0.2 compare_select_fusion
  15.8 0.3 reshape.79
  16.0 0.0 copy-done
  16.0 0.3 convolution_convert_fusion
  16.3 18.3 %gather_fusion = bf16[4096,1024]{1,0:T(8,128)(2,1)} fusion(bf16[256,1024]{1,0:T(8,128)(2,1)S(1)} %convolution_convert_fusion, s32[4096]{0:T(1024)S(1)} %broadcast_clamp_fusion), kind=kCustom, calls=%fused_computation | custom fusion | bytes 16793600 | tf_op jit(solution)/shard_map/gather | solution.py:44
  34.6 13.1 %reshape.78 = bf16[8,128,4,1024]{3,2,1,0:T(4,128)(2,1)} reshape(bf16[4096,1024]{1,0:T(8,128)(2,1)} %gather_fusion) | data formatting | bytes 16777216 | tf_op jit(solution)/shard_map/gather | solution.py:44
  47.7 8.4 %copy.18 = bf16[8,128,4,1024]{3,2,0,1:T(4,128)(2,1)} copy(bf16[8,128,4,1024]{3,2,1,0:T(4,128)(2,1)} %reshape.78) | data formatting | bytes 16777216 | tf_op jit(solution)/shard_map/gather | solution.py:44
  56.1 17.0 %all-to-all-start = ((bf16[8,128,4,1024]{3,2,0,1:T(4,128)(2,1)}), bf16[8,128,4,1024]{3,2,0,1:T(4,128)(2,1)}, u32[]{:S(2)}, u32[]{:S(2)}) async-start(bf16[8,128,4,1024]{3,2,0,1:T(4,128)(2,1)} %copy.18), calls=%async_computation | async-start | bytes 16777216 | tf_op jit(solution)/shard_map/all_to_all | solution.py:45
  73.1 0.0 copy-done.5
  73.2 186.1 %all-to-all-done = bf16[8,128,4,1024]{3,2,0,1:T(4,128)(2,1)} async-done(((bf16[8,128,4,1024]{3,2,0,1:T(4,128)(2,1)}), bf16[8,128,4,1024]{3,2,0,1:T(4,128)(2,1)}, u32[]{:S(2)}, u32[]{:S(2)}) %all-to-all-start) | async-done | bytes 8388640 | tf_op jit(solution)/shard_map/all_to_all | solution.py:45
  259.3 8.1 %copy.19 = bf16[8,128,4,1024]{3,2,1,0:T(4,128)(2,1)} copy(bf16[8,128,4,1024]{3,2,0,1:T(4,128)(2,1)} %all-to-all-done) | data formatting | bytes 16777216 | tf_op jit(solution)/shard_map/all_to_all | solution.py:45
  267.4 12.5 %reshape.70 = bf16[8,512,1024]{2,1,0:T(8,128)(2,1)} reshape(bf16[8,128,4,1024]{3,2,1,0:T(4,128)(2,1)} %copy.19) | data formatting | bytes 16777216 | tf_op jit(solution)/shard_map/reshape | solution.py:45
  279.9 7.0 %multiply_reduce_fusion = (f32[8,512]{1,0:T(8,128)S(1)}, f32[8,512,256]{1,2,0:T(8,128)S(1)}) fusion(bf16[8,512,1024]{2,1,0:T(8,128)(2,1)} %reshape.70, bf16[8,256,1024]{2,1,0:T(8,128)(2,1)} %bitcast.39), kind=kOutput, calls=%fused_computation.10 | convolution fusion | flops 2149576704 | bytes 16793600 | tf_op jit(solution)/shard_map/kmd,kjd->kmj/dot_general | solution.py:14
  286.9 0.0 copy-start.4
  286.9 2.0 copy-done.4
  288.9 0.7 exponential_reduce_fusion
  289.6 0.8 copy.23
  290.5 7.2 %all-to-all-start.2 = ((f32[8,128,4]{0,2,1:T(4,128)}), f32[8,128,4]{0,2,1:T(4,128)S(1)}, u32[]{:S(2)}, u32[]{:S(2)}) async-start(f32[8,128,4]{0,2,1:T(4,128)} %bitcast.7), calls=%async_computation.2 | async-start | bytes 524288 | tf_op jit(solution)/shard_map/all_to_all | solution.py:59
  297.6 0.1 iota_compare_fusion.3
  297.7 0.1 copy.22
  297.8 0.1 reshape.87
  297.9 0.8 copy.20
  298.7 11.6 %all-to-all-done.2 = f32[8,128,4]{0,2,1:T(4,128)S(1)} async-done(((f32[8,128,4]{0,2,1:T(4,128)}), f32[8,128,4]{0,2,1:T(4,128)S(1)}, u32[]{:S(2)}, u32[]{:S(2)}) %all-to-all-start.2) | async-done | bytes 16416 | tf_op jit(solution)/shard_map/all_to_all | solution.py:59
  310.3 6.3 %all-to-all-start.1 = ((f32[8,128,4]{0,2,1:T(4,128)}), f32[8,128,4]{0,2,1:T(4,128)S(1)}, u32[]{:S(2)}, u32[]{:S(2)}) async-start(f32[8,128,4]{0,2,1:T(4,128)} %bitcast.3), calls=%async_computation.1 | async-start | bytes 524288 | tf_op jit(solution)/shard_map/all_to_all | solution.py:52
  316.7 0.0 reduce-scatter.5.cloned.1.call-start
  316.7 0.1 lt.46
  316.9 0.8 copy.24
  317.7 11.5 %all-to-all-done.1 = f32[8,128,4]{0,2,1:T(4,128)S(1)} async-done(((f32[8,128,4]{0,2,1:T(4,128)}), f32[8,128,4]{0,2,1:T(4,128)S(1)}, u32[]{:S(2)}, u32[]{:S(2)}) %all-to-all-start.1) | async-done | bytes 16416 | tf_op jit(solution)/shard_map/all_to_all | solution.py:52
  329.2 0.8 copy.21
  330.0 2.8 gather_fusion.2
  332.8 2.8 gather_fusion.1
  335.7 0.1 bitcast_reduce_fusion
  335.8 0.1 reduce_max.22
  335.9 0.2 fusion.8
  336.1 0.1 log.10
  336.2 0.0 copy-start.2
  336.2 25.7 %gather_fusion.3 = f32[4096]{0:T(1024)S(1)} fusion(f32[256]{0:T(256)S(1)} %add_select_fusion.1, s32[4096]{0:T(1024)S(1)} %broadcast_clamp_fusion), kind=kCustom, calls=%fused_computation.3 | custom fusion | bytes 49152 | tf_op jit(solution)/shard_map/gather | solution.py:76
  362.0 0.0 copy-done.2
  362.0 0.5 reshape.102
  362.5 0.9 copy.25
  363.4 18.1 %all_to_all.20 = f32[8,128,4]{0,2,1:T(4,128)S(1)} all-to-all(f32[8,128,4]{0,2,1:T(4,128)S(1)} %copy.25), channel_id=1, replica_groups=mesh['dp'=128,'rep'=2] {'dp'}, dimensions={1} | all-to-all | bytes 32768 | tf_op jit(solution)/shard_map/all_to_all | solution.py:77
  381.5 0.1 copy.26
  381.6 3.0 fusion
  384.5 0.6 broadcast_in_dim.11
  385.1 0.0 reduce-scatter.5.cloned.1.call-update
  385.1 0.0 reduce-scatter.3.cloned.1.call-start
  385.2 10.2 %fusion.2 = f32[8,256,1024]{2,1,0:T(8,128)} fusion(bf16[8,512,1024]{2,1,0:T(8,128)(2,1)} %reshape.70, f32[8,512,256]{1,2,0:T(8,128)} %copy-done.4, f32[8,512]{1,0:T(8,128)S(1)} %copy.26), kind=kOutput, calls=%fused_computation.11 | convolution fusion | flops 2150629376 | bytes 20987904 | tf_op jit(solution)/shard_map/kmj,kmd->kjd/dot_general | solution.py:84
  395.4 0.0 reduce-scatter.3.cloned.1.call-update
  395.5 0.6 copy-done.6
  396.1 0.0 copy-done.3
  396.1 1.8 gather_fusion.4
  397.9 0.7 add_bitcast_fusion
  398.6 24.1 %reduce-scatter.3.cloned.1.call-done = f32[8,256,512]{2,1,0:T(8,128)} async-done(((f32[8,256,1024]{2,1,0:T(8,128)}), f32[8,256,512]{2,1,0:T(8,128)}) %reduce-scatter.3.cloned.1.call-update) | async-done | bytes 4194320 | tf_op jit(solution)/shard_map/reduce_scatter | solution.py:88
  422.7 5.5 %add_divide_fusion = f32[8,256,512]{2,1,0:T(8,128)} fusion(f32[8,256,512]{2,1,0:T(8,128)} %reduce-scatter.3.cloned.1.call-done, f32[8,256]{1,0:T(8,128)S(1)} %add_bitcast_fusion, bf16[8,256,1024]{2,1,0:T(8,128)(2,1)} %bitcast.40, s32[]{:T(128)S(6)} %select_n.33), kind=kLoop, calls=%fused_computation.5 | loop fusion | flops 4194304 | bytes 10493956 | tf_op jit(solution)/shard_map/div | solution.py:94
  428.2 0.0 copy-done.1
  (15 shorter events, 0.1 us)
Async XLA Ops:
  7.2 8.9 %copy-start = (bf16[128,1024]{1,0:T(8,128)(2,1)S(1)}, bf16[128,1024]{1,0:T(8,128)(2,1)}, u32[]{:S(2)}) copy-start(bf16[128,1024]{1,0:T(8,128)(2,1)} %param.4) | copy-start | bytes 786436
  56.1 17.0 %copy-start.5 = (s32[64,16]{0,1:T(8,128)S(1)}, s32[64,16]{0,1:T(8,128)}, u32[]{:S(2)}) copy-start(s32[64,16]{0,1:T(8,128)} %param.6) | copy-start | bytes 12292
  56.1 203.2 %all-to-all-start = ((bf16[8,128,4,1024]{3,2,0,1:T(4,128)(2,1)}), bf16[8,128,4,1024]{3,2,0,1:T(4,128)(2,1)}, u32[]{:S(2)}, u32[]{:S(2)}) async-start(bf16[8,128,4,1024]{3,2,0,1:T(4,128)(2,1)} %copy.18), calls=%async_computation | async-start | bytes 16777216 | tf_op jit(solution)/shard_map/all_to_all | solution.py:45
  286.9 2.0 copy-start.4
  290.5 19.9 %all-to-all-start.2 = ((f32[8,128,4]{0,2,1:T(4,128)}), f32[8,128,4]{0,2,1:T(4,128)S(1)}, u32[]{:S(2)}, u32[]{:S(2)}) async-start(f32[8,128,4]{0,2,1:T(4,128)} %bitcast.7), calls=%async_computation.2 | async-start | bytes 524288 | tf_op jit(solution)/shard_map/all_to_all | solution.py:59
  310.3 18.9 %all-to-all-start.1 = ((f32[8,128,4]{0,2,1:T(4,128)}), f32[8,128,4]{0,2,1:T(4,128)S(1)}, u32[]{:S(2)}, u32[]{:S(2)}) async-start(f32[8,128,4]{0,2,1:T(4,128)} %bitcast.3), calls=%async_computation.1 | async-start | bytes 524288 | tf_op jit(solution)/shard_map/all_to_all | solution.py:52
  316.7 81.2 %reduce-scatter.5.cloned.1.call-start = ((), (), s32[]{:S(2)}) async-start(), calls=%async_computation.7 | async-start | bytes 24576 | tf_op jit(solution)/shard_map/reduce_scatter | solution.py:89
  336.2 25.8 %copy-start.2 = (f32[256]{0:T(256)}, f32[256]{0:T(256)S(1)}, u32[]{:S(2)}) copy-start(f32[256]{0:T(256)S(1)} %log.10) | copy-start | bytes 3076
  385.1 37.6 %reduce-scatter.3.cloned.1.call-start = ((), (), s32[]{:S(2)}) async-start(), calls=%async_computation.6 | async-start | bytes 12582912 | tf_op jit(solution)/shard_map/reduce_scatter | solution.py:88
  395.4 0.7 copy-start.6
  395.4 0.7 copy-start.3
  397.9 30.3 %copy-start.1 = (bf16[128,1024]{1,0:T(8,128)(2,1)S(1)}, bf16[128,1024]{1,0:T(8,128)(2,1)}, u32[]{:S(2)}) copy-start(bf16[128,1024]{1,0:T(8,128)(2,1)} %param.4) | copy-start | bytes 786436
Sparse Core Ops, SparseCore 0:
  385.3 11.5 reduce-scatter.4
  399.4 23.2 reduce-scatter.2
where the time goes:
time: 436 us; the launch traced here: 435 us
  waiting for transfers between devices  233 us (53%)
  local copies, waits for them, and re-layouts  103 us (24%)
  starting transfers between devices  30.6 us (7%)
  blocking collectives  18.1 us (4%)
  other arithmetic  17.8 us (4%)
  matrix products  17.5 us (4%)
  between operations  14.3 us (3%)
    all_to_all x1, waiting for transfers between devices, local(): lax.all_to_all(outgoing, 'dp', split_axis=1, concat_axis=1, tiled=True)  186 us
    gather x3, local copies, waits for them, and re-layouts, local(): outgoing = packed[send_order]  39.8 us
    gather x3, local copies, waits for them, and re-layouts, local(): norm_blocks = lognorm.reshape(-1)[send_order]  27.1 us
    reduce_scatter x1, waiting for transfers between devices, local(): lax.psum_scatter(sum_rows, 'rep', scatter_dimension=2, tiled=True)  24.1 us
    all_to_all x1, blocking collectives, local(): lax.all_to_all(norm_blocks, 'dp', split_axis=1, concat_axis=1, tiled=True)  18.1 us
    all_to_all x1, starting transfers between devices, local(): lax.all_to_all(outgoing, 'dp', split_axis=1, concat_axis=1, tiled=True)  17 us
    reshape x1, local copies, waits for them, and re-layouts, local(): lax.all_to_all(outgoing, 'dp', split_axis=1, concat_axis=1, tiled=True)  12.5 us
    all_to_all x1, waiting for transfers between devices, local(): lax.all_to_all(block_sum.reshape(own_blocks, dp_size, capacity), 'dp', sp...  11.6 us
  transfers between devices with their start and end apart: 5, of which 4 were waited for; matrix products, arithmetic and copies ran while one was open for 3% of the time, Pallas kernels for 0%

commit v1 on v0

v1 whole, which is shorter than its diff:
```python
import math

import jax
import jax.numpy as jnp
from jax import lax
from jax.experimental import pallas as pl
from jax.experimental.pallas import tpu as pltpu
from jax.sharding import PartitionSpec as P

BETA = 3.0
LAMBDA = 0.25
EMPTY_NORM = 1e30
NONE_MAX = -1e30
MESH = pl.DeviceIdType.MESH

NY, NX, NZ, NC = 4, 4, 8, 2
ROWS = 128
D = 1024
HALF = 512
BS = 256
OWN = 4
CAP = 4
F32 = jnp.float32
BF16 = jnp.bfloat16


def kernel(
    emb, par, bl, cent, out, spread,
    raw, slz, slp, pk, inc, ce, e_sc, ms, ss, stt, rs, tz, lt, lr, wb, fr, keys, pbq,
    s_zs, s_zr, s_as, s_ar, s_slzs, s_slzr, s_slps, s_slpr, s_ps, s_pr, s_loc, s_ce,
    s_sts, s_str, s_tzs, s_tzr, s_ls, s_lr, s_fs, s_fr, s_fl,
):
    dp = lax.axis_index("dp")
    c = lax.axis_index("rep")
    y = dp // 32
    x = (dp // 8) % 4
    z = dp % 8

    def chip(yy, xx, zz):
        return (yy * 4 + xx) * 8 + zz

    def zdev(dz):
        return (chip(y, x, (z + dz) % 8), c)

    def adev(p, k, dc=0):
        return (chip((y + k) % 4, x, z) if p == 0 else chip(y, (x + k) % 4, z), c)

    def bdev(p, k, dc):
        cc = (c + dc) % 2
        return (chip(y, (x + k) % 4, z) if p == 0 else chip((y + k) % 4, x, z), cc)

    def plane(t):
        yy, xx, cc = (y + t // 8) % 4, (x + (t // 2) % 4) % 4, (c + t % 2) % 2
        return (chip(yy, xx, z), cc), (yy * 4 + xx) * 2 + cc

    my_u = (y * 4 + x) * 2 + c

    ce_copy = pltpu.make_async_copy(cent.at[pl.ds(c * 1024, 1024)], ce, s_ce)
    ce_copy.start()

    barrier = pltpu.get_barrier_semaphore()

    def greet(t, carry):
        dev, _ = plane(t)
        pl.semaphore_signal(barrier, 1, device_id=dev, device_id_type=MESH)
        return carry

    lax.fori_loop(1, 32, greet, 0)
    for dz in range(1, 8):
        pl.semaphore_signal(barrier, 1, device_id=zdev(dz), device_id_type=MESH)
    for p in range(2):
        raw[p, 0, 1] = emb[:, p * HALF:(p + 1) * HALF]
    pl.semaphore_wait(barrier, 38)

    def zsend(p, pos, step):
        to = (pos + 1) % 8 if step < 0 else (pos - 1) % 8
        pltpu.make_async_remote_copy(
            src_ref=raw.at[p, 0, pos], dst_ref=raw.at[p, 0, to],
            send_sem=s_zs.at[p], recv_sem=s_zr.at[p, to],
            device_id=zdev(step), device_id_type=MESH,
        ).start()

    def asend(p, pos):
        for k in (1, 3, 2):
            to = (-k) % 4
            pltpu.make_async_remote_copy(
                src_ref=raw.at[p, 0, pos], dst_ref=raw.at[p, to, pos],
                send_sem=s_as.at[p], recv_sem=s_ar.at[p, to, pos // 4],
                device_id=adev(p, k), device_id_type=MESH,
            ).start()

    def zwait(p, pos):
        pltpu.make_async_copy(raw.at[p, 0, pos], raw.at[p, 0, pos], s_zr.at[p, pos]).wait()

    for p in range(2):
        zsend(p, 1, -1)
        zsend(p, 1, 1)
    for p in range(2):
        asend(p, 1)

    par_row = par[0:1, :]
    sub = lax.broadcasted_iota(jnp.int32, (ROWS, ROWS), 0)
    lane = lax.broadcasted_iota(jnp.int32, (ROWS, ROWS), 1)
    par_wide = jnp.broadcast_to(par_row, (ROWS, ROWS))
    par_col = jnp.sum(jnp.where(sub == lane, par_wide, 0.0), axis=1, keepdims=True)
    earlier = jnp.where((par_col == par_wide) & (sub < lane), 1.0, 0.0)
    slot_row = par_row * CAP + jnp.sum(earlier, axis=0, keepdims=True)
    slot_col = jnp.sum(
        jnp.where(sub == lane, jnp.broadcast_to(slot_row, (ROWS, ROWS)), 0.0), axis=1, keepdims=True
    )
    slz[1, 0:8, :] = jnp.broadcast_to(slot_row, (8, 128))
    code = ((lane // 32) * CAP + lane % CAP).astype(F32)
    for p4 in range(16):
        hit = jnp.where(slot_col == code + float(16 * p4), 1.0, 0.0)
        slz[1, 8 + p4:9 + p4, :] = jnp.sum(hit, axis=0, keepdims=True)
    for dz in range(1, 8):
        to = (1 - dz) % 8
        pltpu.make_async_remote_copy(
            src_ref=slz.at[1], dst_ref=slz.at[to], send_sem=s_slzs, recv_sem=s_slzr,
            device_id=zdev(dz), device_id_type=MESH,
        ).start()

    def lookup(ids):
        n = ids.shape[0]
        acc = jnp.zeros((n, 128), F32)
        for ch in range(8):
            place = lax.broadcasted_iota(jnp.int32, (1, 128), 1) + ch * 128
            acc += jnp.where(ids == bl[ch:ch + 1, :], (place // 16).astype(F32), 0.0)
        return jnp.sum(acc, axis=1, keepdims=True)

    row = lax.broadcasted_iota(jnp.int32, (512, 1), 0)
    zz = (row // 4) % 4
    core = (row // 64) % 2
    core = jnp.where(core == 0, c, 1 - c)
    for p in range(2):
        far = row // 128
        where_to = chip(y, (x + far) % 4, z) if p == 0 else chip((y + far) % 4, x, z)
        ids = where_to * 8 + core * 4 + (row // 16) % 4
        keys[p] = jnp.broadcast_to(
            lookup(ids) * CAP + (row % 4).astype(F32) + (zz * 256).astype(F32), (512, 128)
        )
    r128 = lax.broadcasted_iota(jnp.int32, (128, 1), 0)
    peer = r128 % 32
    peer_chip = (peer // 2) * 8 + z
    wide = jnp.zeros((128, 128), F32)
    for q in range(4):
        ids = peer_chip * 8 + (peer % 2) * 4 + (q + 4 - r128 // 32) % 4
        wide = jnp.where(lane // 32 == q, lookup(ids) - float(q), wide)
    pbq[...] = wide

    for p in range(2):
        zwait(p, 2)
        zsend(p, 2, -1)
        zwait(p, 0)
        zsend(p, 0, 1)
    for p in range(2):
        asend(p, 2)
        asend(p, 0)
    pltpu.make_async_copy(slz.at[0:7], slz.at[0:7], s_slzr).wait()
    for p in range(2):
        for k in (1, 3, 2):
            to = (-k) % 4
            pltpu.make_async_remote_copy(
                src_ref=slz.at[:, 0:8, :], dst_ref=slp.at[p, to - 1],
                send_sem=s_slps.at[p], recv_sem=s_slpr.at[p],
                device_id=adev(p, k), device_id_type=MESH,
            ).start()
    for p in range(2):
        zwait(p, 3)
        zsend(p, 3, -1)
        zwait(p, 7)
        zsend(p, 7, 1)
    for p in range(2):
        asend(p, 3)
        asend(p, 7)
    for p in range(2):
        zwait(p, 4)
        zwait(p, 6)
        zsend(p, 4, -1) if p == 0 else zsend(p, 6, 1)
    for p in range(2):
        asend(p, 4)
        asend(p, 6)
    for p in range(2):
        zwait(p, 5)
        asend(p, 5)

    for p in range(2):
        pltpu.make_async_copy(slp.at[p], slp.at[p], s_slpr.at[p]).wait()

    def pack(p, g, k):
        n = g * 4 + k
        if k > 0:
            pltpu.make_async_copy(
                raw.at[p, k, pl.ds(4 * g, 4)], raw.at[p, k, pl.ds(4 * g, 4)], s_ar.at[p, k, g]
            ).wait()
        key = keys[p][:, 0:1]
        picks = []
        for w in range(4):
            s_row = slz[4 * g + w, 0:1, :] if k == 0 else slp[p, k - 1, 4 * g + w, 0:1, :]
            picks.append(jnp.where(key == s_row + float(256 * w), 1.0, 0.0).astype(BF16))
        pick = jnp.concatenate(picks, axis=1)
        rows = raw[p, k, 4 * g:4 * g + 4].reshape(512, HALF)
        packed = jnp.dot(pick, rows, preferred_element_type=F32).astype(BF16)
        pk[p, n] = packed.reshape(8, OWN, 16, HALF)
        u = (((y + k) % 4) * 4 + x) * 2 + c if p == 0 else (y * 4 + (x + k) % 4) * 2 + c
        off = pl.multiple_of((u % 8) * 128 + (u // 8) * 32 + g * 16, 16)
        dst = inc.at[:, pl.ds(off, 16), p * HALF:(p + 1) * HALF]
        for far in (1, 3, 2, 0):
            for dc in range(2):
                i = far * 2 + dc
                if i == 0:
                    pltpu.make_async_copy(pk.at[p, n, 0], dst, s_loc.at[p]).start()
                else:
                    pltpu.make_async_remote_copy(
                        src_ref=pk.at[p, n, i], dst_ref=dst,
                        send_sem=s_ps.at[p], recv_sem=s_pr.at[p],
                        device_id=bdev(p, far, dc), device_id_type=MESH,
                    ).start()

    for g in range(2):
        for k in (0, 1, 3, 2):
            for p in range(2):
                pack(p, g, k)

    ce_copy.wait()
    for p in range(2):
        got = inc.at[:, 0:896, p * HALF:(p + 1) * HALF]
        pltpu.make_async_copy(got, got, s_pr.at[p]).wait()
        pltpu.make_async_copy(pk.at[p, :, 0], pk.at[p, :, 0], s_loc.at[p]).wait()

    scale = BETA / math.sqrt(D)

    def score(j, carry):
        for n in range(4):
            s = lax.dot_general(
                ce[pl.ds(pl.multiple_of(j * BS, BS), BS), :], inc[j, n * 256:(n + 1) * 256, :],
                (((1,), (1,)), ((), ())), preferred_element_type=F32,
            ) * scale
            top = jnp.max(s, axis=0, keepdims=True)
            e = jnp.exp(s - top)
            e_sc[j, n] = e
            total = jnp.sum(e, axis=0, keepdims=True)
            for h in range(2):
                ms[j, 2 * n + h:2 * n + h + 1, :] = top[:, h * 128:(h + 1) * 128]
                ss[j, 2 * n + h:2 * n + h + 1, :] = total[:, h * 128:(h + 1) * 128]
        return carry

    lax.fori_loop(0, OWN, score, 0)

    group = lax.broadcasted_iota(jnp.int32, (8, 128), 1) // 32
    for q in range(4):
        tops, totals = ms[q], ss[q]
        for j in range(4):
            if j != q:
                turn = (32 * (j - q)) % 128
                tops = jnp.where(group == j, pltpu.roll(ms[j], turn, 1), tops)
                totals = jnp.where(group == j, pltpu.roll(ss[j], turn, 1), totals)
        for v in range(8):
            stt[8 * q + v, 0:1, :] = tops[v:v + 1, :]
            stt[8 * q + v, 1:2, :] = totals[v:v + 1, :]
    rs[my_u] = stt[my_u]

    def send_stats(t, carry):
        dev, u = plane(t)
        pltpu.make_async_remote_copy(
            src_ref=stt.at[u], dst_ref=rs.at[my_u], send_sem=s_sts, recv_sem=s_str,
            device_id=dev, device_id_type=MESH,
        ).start()
        return carry

    lax.fori_loop(1, 32, send_stats, 0)
    pltpu.make_async_copy(rs.at[0:31], rs.at[0:31], s_str).wait()

    m_in = jnp.concatenate([rs[d, 0:1, :] for d in range(32)], axis=0)
    s_in = jnp.concatenate([rs[d, 1:2, :] for d in range(32)], axis=0)
    m_all = jnp.concatenate([m_in] + [pltpu.roll(m_in, 32 * k, 1) for k in (1, 2, 3)], axis=0)
    s_all = jnp.concatenate([s_in] + [pltpu.roll(s_in, 32 * k, 1) for k in (1, 2, 3)], axis=0)
    owner = pbq[...]
    m_back = jnp.zeros((128, 128), F32)
    for p4 in range(16):
        mine = owner == float(4 * p4)
        top = jnp.max(jnp.where(mine, m_all, NONE_MAX), axis=0, keepdims=True)
        tz[0, 0, p4:p4 + 1, :] = top
        m_back = jnp.where(mine, top, m_back)
    z_all = s_all * jnp.exp(m_all - m_back)
    for p4 in range(16):
        mine = owner == float(4 * p4)
        tz[0, 1, p4:p4 + 1, :] = jnp.sum(jnp.where(mine, z_all, 0.0), axis=0, keepdims=True)

    for dz in range(1, 8):
        pltpu.make_async_remote_copy(
            src_ref=tz.at[0], dst_ref=tz.at[8 - dz], send_sem=s_tzs, recv_sem=s_tzr,
            device_id=zdev(dz), device_id_type=MESH,
        ).start()
    place = lax.broadcasted_iota(jnp.int32, (16, 128), 1) % 32
    filled = jnp.zeros((16, 128), F32)
    for pos in range(8):
        filled = jnp.where(place // 4 == pos, slz[pos, 8:24, :], filled)
    pltpu.make_async_copy(tz.at[1:8], tz.at[1:8], s_tzr).wait()

    def aligned(dz, what):
        t = tz[dz, what]
        if dz == 0:
            return t
        turn = 4 * dz
        return jnp.where(place >= turn, pltpu.roll(t, turn, 1), pltpu.roll(t, 96 + turn, 1))

    tops = [aligned(dz, 0) for dz in range(8)]
    highest = tops[0]
    for t in tops[1:]:
        highest = jnp.maximum(highest, t)
    summed = jnp.zeros((16, 128), F32)
    for dz in range(8):
        summed += aligned(dz, 1) * jnp.exp(tops[dz] - highest)
    log_total = jnp.log(summed)
    norm = jnp.where(filled > 0.5, highest + log_total, EMPTY_NORM)

    turned = jnp.zeros((128, 128), F32)
    for p4 in range(16):
        turned = jnp.where(owner == float(4 * p4), norm[p4:p4 + 1, :], turned)
    back = turned[0:32]
    for k in (1, 2, 3):
        back += pltpu.roll(turned[32 * k:32 * k + 32], 128 - 32 * k, 1)
    for d in range(32):
        lt[d, 0:1, :] = back[d:d + 1, :]
    lr[my_u] = lt[my_u]

    def send_norm(t, carry):
        dev, u = plane(t)
        pltpu.make_async_remote_copy(
            src_ref=lt.at[u], dst_ref=lr.at[my_u], send_sem=s_ls, recv_sem=s_lr,
            device_id=dev, device_id_type=MESH,
        ).start()
        return carry

    lax.fori_loop(1, 32, send_norm, 0)

    slot_i = slz[1, 0:1, :].astype(jnp.int32)
    lane_of = ((slot_i // 4) % 4) * 32 + 4 + slot_i % 4
    choose = jnp.where(sub == jnp.broadcast_to(lane_of, (128, 128)), 1.0, 0.0)
    by_lane = jnp.dot(
        log_total, choose, preferred_element_type=F32, precision=lax.Precision.HIGHEST
    )
    p4_row = lax.broadcasted_iota(jnp.int32, (16, 128), 0)
    spread[0:1, :] = jnp.sum(
        jnp.where(p4_row == jnp.broadcast_to(slot_i // 16, (16, 128)), by_lane, 0.0),
        axis=0, keepdims=True,
    )

    pltpu.make_async_copy(lr.at[0:31], lr.at[0:31], s_lr).wait()

    for q in range(4):
        got = jnp.concatenate([lr[8 * q + v, 0:1, :] for v in range(8)], axis=0)
        for j in range(4):
            turn = (32 * (q - j)) % 128
            turned = got if turn == 0 else pltpu.roll(got, turn, 1)
            ss[j] = jnp.where(group == q, turned, ss[j])
    own_col = pl.multiple_of(c * HALF, HALF)
    far_col = pl.multiple_of((1 - c) * HALF, HALF)

    def update(j, carry):
        factor = jnp.exp(ms[j] - ss[j])
        mass = jnp.zeros((BS, 128), F32)
        for n in range(4):
            for h in range(2):
                v = 2 * n + h
                w = e_sc[j, n, :, h * 128:(h + 1) * 128] * factor[v:v + 1, :]
                mass += w
                wb[:, v * 128:(v + 1) * 128] = w.astype(BF16)
        denom = jnp.sum(mass, axis=1, keepdims=True) + LAMBDA
        rows = pl.ds(pl.multiple_of(j * BS, BS), BS)
        at = pl.ds(pl.multiple_of((c * OWN + j) * BS, BS), BS)
        for i, col in ((1, far_col), (0, own_col)):
            sums = jnp.dot(wb[...], inc[j, :, pl.ds(col, HALF)], preferred_element_type=F32)
            prev = ce[rows, pl.ds(col, HALF)].astype(F32)
            fr[i, rows, :] = (sums + LAMBDA * prev) / denom
            if i == 1:
                pltpu.make_async_remote_copy(
                    src_ref=fr.at[1, rows], dst_ref=out.at[at], send_sem=s_fs, recv_sem=s_fr,
                    device_id=(dp, 1 - c), device_id_type=MESH,
                ).start()
            else:
                pltpu.make_async_copy(fr.at[0, rows], out.at[at], s_fl).start()
        return carry

    lax.fori_loop(0, OWN, update, 0)

    pltpu.make_async_copy(fr.at[0], fr.at[0], s_fl).wait()
    pltpu.make_async_copy(fr.at[1], fr.at[1], s_fs).wait()
    pltpu.make_async_copy(fr.at[1], fr.at[1], s_fr).wait()
    for p in range(2):
        pltpu.make_async_copy(raw.at[p, 0, 0:7], raw.at[p, 0, 0:7], s_zs.at[p]).wait()
        pltpu.make_async_copy(raw.at[p, 1:4], raw.at[p, 1:4], s_as.at[p]).wait()
        pltpu.make_async_copy(slp.at[p], slp.at[p], s_slps.at[p]).wait()
        pltpu.make_async_copy(pk.at[p, :, 1:8], pk.at[p, :, 1:8], s_ps.at[p]).wait()
    pltpu.make_async_copy(slz.at[0:7], slz.at[0:7], s_slzs).wait()
    pltpu.make_async_copy(stt.at[0:31], stt.at[0:31], s_sts).wait()
    pltpu.make_async_copy(tz.at[1:8], tz.at[1:8], s_tzs).wait()
    pltpu.make_async_copy(lt.at[0:31], lt.at[0:31], s_ls).wait()


def local(embeddings, parents, block_lists, centroids):
    dma, vmem = pltpu.SemaphoreType.DMA, pltpu.VMEM
    fresh, spread = pl.pallas_call(
        kernel,
        out_shape=(
            jax.ShapeDtypeStruct((2 * OWN * BS, HALF), F32),
            jax.ShapeDtypeStruct((1, ROWS), F32),
        ),
        in_specs=[
            pl.BlockSpec(memory_space=vmem),
            pl.BlockSpec(memory_space=vmem),
            pl.BlockSpec(memory_space=vmem),
            pl.BlockSpec(memory_space=pl.ANY),
        ],
        out_specs=(pl.BlockSpec(memory_space=pl.ANY), pl.BlockSpec(memory_space=vmem)),
        scratch_shapes=[
            vmem((2, 4, 8, ROWS, HALF), BF16),
            vmem((8, 24, 128), F32),
            vmem((2, 3, 8, 8, 128), F32),
            vmem((2, 8, 8, OWN, 16, HALF), BF16),
            vmem((OWN, 1024, D), BF16),
            vmem((OWN * BS, D), BF16),
            vmem((OWN, 4, BS, 256), F32),
            vmem((OWN, 8, 128), F32),
            vmem((OWN, 8, 128), F32),
            vmem((32, 8, 128), F32),
            vmem((32, 8, 128), F32),
            vmem((8, 2, 16, 128), F32),
            vmem((32, 8, 128), F32),
            vmem((32, 8, 128), F32),
            vmem((BS, 1024), BF16),
            vmem((2, OWN * BS, HALF), F32),
            vmem((2, 512, 128), F32),
            vmem((128, 128), F32),
            dma((2,)), dma((2, 8)), dma((2,)), dma((2, 4, 2)),
            dma, dma, dma((2,)), dma((2,)), dma((2,)), dma((2,)), dma((2,)), dma,
            dma, dma, dma, dma, dma, dma, dma, dma, dma,
        ],
        compiler_params=pltpu.CompilerParams(
            collective_id=0, has_side_effects=True, vmem_limit_bytes=56 * 1024 * 1024
        ),
        cost_estimate=pl.CostEstimate(
            flops=8_000_000_000, bytes_accessed=10_000_000, transcendentals=1_000_000
        ),
        name="kmeans_step",
    )(
        embeddings,
        parents.astype(F32).reshape(1, ROWS),
        block_lists.reshape(8, 128),
        centroids,
    )
    return fresh, spread.reshape(ROWS)


def solution(mesh):
    placed = (P(("dp", "rep"), None), P(("dp", "rep")), P(), P("dp", None))
    return jax.shard_map(
        local,
        mesh=mesh,
        in_specs=placed,
        out_specs=(P("dp", "rep"), P(("dp", "rep"))),
        check_vma=False,
    )
```

time: 436 us -> 143 us (0.33)
  waiting for transfers between devices: 233 us -> 0 us
  Pallas kernels: 0 us -> 135 us
  local copies, waits for them, and re-layouts: 103 us -> 6.61 us
  starting transfers between devices: 30.6 us -> 0 us
  blocking collectives: 18.1 us -> 0 us
  matrix products: 17.5 us -> 0 us
  other arithmetic: 17.8 us -> 1.17 us
  between operations: 14.3 us -> 0.65 us
    all_to_all x3 -> x0, waiting for transfers between devices: 209 us -> none  [the longest x1 186 us: local(): lax.all_to_all(outgoing, 'dp', split_axis=1, concat_axis=1, tiled=True)]
    pallas_call x0 -> x1, Pallas kernels: none -> 135 us  [local(): pl.pallas_call(kernel, out_shape=(jax.ShapeDtypeStruct((2 * OWN * BS, HAL...]
    gather x9 -> x0, local copies, waits for them, and re-layouts: 74.3 us -> none  [the longest x3 39.8 us: local(): outgoing = packed[send_order]]
    all_to_all x3 -> x0, starting transfers between devices: 30.5 us -> none  [the longest x1 17 us: local(): lax.all_to_all(outgoing, 'dp', split_axis=1, concat_axis=1, tiled=True)]
    reduce_scatter x2 -> x0, waiting for transfers between devices: 24.1 us -> none  [the longest x1 24.1 us: local(): lax.psum_scatter(sum_rows, 'rep', scatter_dimension=2, tiled=True)]
    all_to_all x1 -> x0, blocking collectives: 18.1 us -> none  [local(): lax.all_to_all(norm_blocks, 'dp', split_axis=1, concat_axis=1, tiled=True)]
    dot_general x3 -> x0, matrix products: 17.5 us -> none  [the longest x1 10.2 us: local(): jnp.einsum('kmj,kmd->kjd', weights, incoming, preferred_element_type=jnp....]
    reshape x2 -> x1, local copies, waits for them, and re-layouts: 12.6 us -> 0.67 us  [local(): block_lists.reshape(8, 128)]
  transfers between devices with their start and end apart: 5 -> 0, of which waited for: 4 -> 0; matrix products, arithmetic and copies ran while one was open for 3% -> 0% of each run, Pallas kernels for 0% -> 0%
where the time goes in v1:
time: 143 us
  Pallas kernels  135 us (94%)
  local copies, waits for them, and re-layouts  6.61 us (5%)
    pallas_call x1, Pallas kernels, local(): pl.pallas_call(kernel, out_shape=(jax.ShapeDtypeStruct((2 * OWN * BS, HAL...  135 us
    unnamed x5, local copies, waits for them, and re-layouts  5.93 us

profile of v1, /device:TPU:1, one launch (start us, length us, event | category | flops | bytes accessed | tf_op | source)
XLA Modules:
  0.0 143.2 jit_solution(5190193144448278270)
XLA Ops:
  0.6 1.2 convert_bitcast_fusion.par
  1.8 0.8 copy.7
  2.6 0.7 reshape.14.bl
  3.2 134.8 %kmeans_step.1 = (f32[2048,512]{1,0:T(8,128)}, f32[1,128]{1,0:T(1,128)}) custom-call(bf16[128,1024]{1,0:T(8,128)(2,1)} %emb.1, f32[1,128]{1,0:T(1,128)} %convert_bitcast_fusion.par, s32[8,128]{1,0:T(8,128)} %reshape.14.bl, bf16[2048,1024]{1,0:T(8,128)(2,1)} %cent.1), custom_call_target="tpu_custom_call" | custom-call | flops 8000000000 | bytes 10000000 | tf_op jit(solution)/shard_map/kmeans_step/pallas_call | solution.py:404
  138.0 0.0 copy-start
  138.1 4.6 %copy.10 = f32[2048,512]{1,0:T(8,128)} copy(f32[2048,512]{1,0:T(8,128)} %get-tuple-element.8) | data formatting | bytes 8388608
  142.7 0.0 copy-done
  142.7 0.5 copy.11
Async XLA Ops:
  138.0 4.7 %copy-start = (f32[1,128]{1,0:T(1,128)S(1)}, f32[1,128]{1,0:T(1,128)}, u32[]{:S(2)}) copy-start(f32[1,128]{1,0:T(1,128)} %get-tuple-element.5) | copy-start | bytes 1540

commit v2 on v1

--- a/solution.py
+++ b/solution.py
@@ -20,6 +20,7 @@
 BS = 256
 OWN = 4
 CAP = 4
+ZF = 96
 F32 = jnp.float32
 BF16 = jnp.bfloat16
 
@@ -27,8 +28,8 @@
 def kernel(
     emb, par, bl, cent, out, spread,
     raw, slz, slp, pk, inc, ce, e_sc, ms, ss, stt, rs, tz, lt, lr, wb, fr, keys, pbq,
-    s_zs, s_zr, s_as, s_ar, s_slzs, s_slzr, s_slps, s_slpr, s_ps, s_pr, s_loc, s_ce,
-    s_sts, s_str, s_tzs, s_tzr, s_ls, s_lr, s_fs, s_fr, s_fl,
+    s_zs, s_zr, s_as, s_ar, s_bs, s_br, s_ys, s_yr, s_slzs, s_slzr, s_slps, s_slpr, s_ps, s_pr, s_loc, s_ce,
+    s_sts, s_str, s_tzs, s_tzr, s_ls, s_lr, s_fs, s_fr,
 ):
     dp = lax.axis_index("dp")
     c = lax.axis_index("rep")
@@ -49,9 +50,13 @@
         cc = (c + dc) % 2
         return (chip(y, (x + k) % 4, z) if p == 0 else chip((y + k) % 4, x, z), cc)
 
+    ys = [(y + t) % 4 for t in range(4)]
+    xs = [(x + t) % 4 for t in range(4)]
+    cs = [c, 1 - c]
+
     def plane(t):
-        yy, xx, cc = (y + t // 8) % 4, (x + (t // 2) % 4) % 4, (c + t % 2) % 2
-        return (chip(yy, xx, z), cc), (yy * 4 + xx) * 2 + cc
+        yx = ys[t // 8] * 4 + xs[(t // 2) % 4]
+        return (yx * 8 + z, cs[t % 2]), yx * 2 + cs[t % 2]
 
     my_u = (y * 4 + x) * 2 + c
 
@@ -60,45 +65,74 @@
 
     barrier = pltpu.get_barrier_semaphore()
 
-    def greet(t, carry):
-        dev, _ = plane(t)
-        pl.semaphore_signal(barrier, 1, device_id=dev, device_id_type=MESH)
-        return carry
-
-    lax.fori_loop(1, 32, greet, 0)
+    for t in range(1, 32):
+        pl.semaphore_signal(barrier, 1, device_id=plane(t)[0], device_id_type=MESH)
     for dz in range(1, 8):
         pl.semaphore_signal(barrier, 1, device_id=zdev(dz), device_id_type=MESH)
     for p in range(2):
         raw[p, 0, 1] = emb[:, p * HALF:(p + 1) * HALF]
     pl.semaphore_wait(barrier, 38)
 
+    def send(src, dst, ssem, rsem, dev):
+        pltpu.make_async_remote_copy(
+            src_ref=src, dst_ref=dst, send_sem=ssem, recv_sem=rsem,
+            device_id=dev, device_id_type=MESH,
+        ).start()
+
+    def arrived(ref, sem):
+        pltpu.make_async_copy(ref, ref, sem).wait()
+
+    def step_to(pos, step):
+        return (pos + 1) % 8 if step < 0 else (pos - 1) % 8
+
     def zsend(p, pos, step):
-        to = (pos + 1) % 8 if step < 0 else (pos - 1) % 8
-        pltpu.make_async_remote_copy(
-            src_ref=raw.at[p, 0, pos], dst_ref=raw.at[p, 0, to],
-            send_sem=s_zs.at[p], recv_sem=s_zr.at[p, to],
-            device_id=zdev(step), device_id_type=MESH,
-        ).start()
+        to = step_to(pos, step)
+        send(raw.at[p, 0, pos, 0:ZF], raw.at[p, 0, to, 0:ZF], s_zs.at[p], s_zr.at[p, to], zdev(step))
+
+    def zwait(p, pos):
+        arrived(raw.at[p, 0, pos, 0:ZF], s_zr.at[p, pos])
 
     def asend(p, pos):
+        for k in (1, 3):
+            send(
+                raw.at[p, 0, pos, 0:ZF], raw.at[p, 4 - k, pos, 0:ZF],
+                s_as.at[p], s_ar.at[p, 4 - k, pos], adev(p, k),
+            )
+
+    def afwd(p, pos):
+        cut = 48
+        for k, lo, hi in ((1, 0, cut), (3, cut, ZF)):
+            arrived(raw.at[p, k, pos, 0:ZF], s_ar.at[p, k, pos])
+            send(
+                raw.at[p, k, pos, lo:hi], raw.at[p, 2, pos, lo:hi],
+                s_as.at[p], s_ar.at[p, 2, pos // 4], adev(p, 4 - k),
+            )
+
+    def bsend(p):
         for k in (1, 3, 2):
-            to = (-k) % 4
-            pltpu.make_async_remote_copy(
-                src_ref=raw.at[p, 0, pos], dst_ref=raw.at[p, to, pos],
-                send_sem=s_as.at[p], recv_sem=s_ar.at[p, to, pos // 4],
-                device_id=adev(p, k), device_id_type=MESH,
-            ).start()
-
-    def zwait(p, pos):
-        pltpu.make_async_copy(raw.at[p, 0, pos], raw.at[p, 0, pos], s_zr.at[p, pos]).wait()
-
-    for p in range(2):
+            send(
+                raw.at[p, 0, 1, ZF:ROWS], raw.at[p, 4 - k, 1, ZF:ROWS],
+                s_bs.at[p], s_br.at[p], adev(p, k),
+            )
+
+    def bwait(p):
+        arrived(raw.at[p, 1:4, 1, ZF:ROWS], s_br.at[p])
+
+    def ysend(p, pos, step):
+        to = step_to(pos, step)
+        send(raw.at[p, :, pos, ZF:ROWS], raw.at[p, :, to, ZF:ROWS], s_ys.at[p], s_yr.at[p, to], zdev(step))
+
+    def ywait(p, pos):
+        arrived(raw.at[p, :, pos, ZF:ROWS], s_yr.at[p, pos])
+
+    both = range(2)
+    for p in both:
         zsend(p, 1, -1)
         zsend(p, 1, 1)
-    for p in range(2):
+        bsend(p)
         asend(p, 1)
 
-    par_row = par[0:1, :]
+    par_row = par[0:1, :].astype(F32)
     sub = lax.broadcasted_iota(jnp.int32, (ROWS, ROWS), 0)
     lane = lax.broadcasted_iota(jnp.int32, (ROWS, ROWS), 1)
     par_wide = jnp.broadcast_to(par_row, (ROWS, ROWS))
@@ -120,12 +154,14 @@
             device_id=zdev(dz), device_id_type=MESH,
         ).start()
 
+    lists = jnp.concatenate([bl[0:8, :], bl[8:16, :]], axis=1)
+
     def lookup(ids):
         n = ids.shape[0]
+        which = (lax.broadcasted_iota(jnp.int32, (1, 128), 1) % 64).astype(F32)
         acc = jnp.zeros((n, 128), F32)
         for ch in range(8):
-            place = lax.broadcasted_iota(jnp.int32, (1, 128), 1) + ch * 128
-            acc += jnp.where(ids == bl[ch:ch + 1, :], (place // 16).astype(F32), 0.0)
+            acc += jnp.where(ids == lists[ch:ch + 1, :], which, 0.0)
         return jnp.sum(acc, axis=1, keepdims=True)
 
     row = lax.broadcasted_iota(jnp.int32, (512, 1), 0)
@@ -148,51 +184,68 @@
         wide = jnp.where(lane // 32 == q, lookup(ids) - float(q), wide)
     pbq[...] = wide
 
-    for p in range(2):
+    for p in both:
+        bwait(p)
+        ysend(p, 1, -1)
+        ysend(p, 1, 1)
+    for p in both:
         zwait(p, 2)
         zsend(p, 2, -1)
         zwait(p, 0)
         zsend(p, 0, 1)
-    for p in range(2):
+    for p in both:
         asend(p, 2)
         asend(p, 0)
-    pltpu.make_async_copy(slz.at[0:7], slz.at[0:7], s_slzr).wait()
-    for p in range(2):
+    arrived(slz.at[0:7], s_slzr)
+    for p in both:
         for k in (1, 3, 2):
-            to = (-k) % 4
-            pltpu.make_async_remote_copy(
-                src_ref=slz.at[:, 0:8, :], dst_ref=slp.at[p, to - 1],
-                send_sem=s_slps.at[p], recv_sem=s_slpr.at[p],
-                device_id=adev(p, k), device_id_type=MESH,
-            ).start()
-    for p in range(2):
+            send(slz.at[:, 0:8, :], slp.at[p, 3 - k], s_slps.at[p], s_slpr.at[p], adev(p, k))
+    for p in both:
+        afwd(p, 1)
+    for p in both:
         zwait(p, 3)
         zsend(p, 3, -1)
         zwait(p, 7)
         zsend(p, 7, 1)
-    for p in range(2):
+    for p in both:
         asend(p, 3)
         asend(p, 7)
-    for p in range(2):
+    for p in both:
+        afwd(p, 2)
+        afwd(p, 0)
+    for p in both:
         zwait(p, 4)
         zwait(p, 6)
         zsend(p, 4, -1) if p == 0 else zsend(p, 6, 1)
-    for p in range(2):
+    for p in both:
         asend(p, 4)
         asend(p, 6)
-    for p in range(2):
+    for p in both:
+        ywait(p, 2)
+        ysend(p, 2, -1)
+        ywait(p, 0)
+        ysend(p, 0, 1)
+    for p in both:
+        afwd(p, 3)
+        afwd(p, 7)
+    for p in both:
         zwait(p, 5)
         asend(p, 5)
-
-    for p in range(2):
-        pltpu.make_async_copy(slp.at[p], slp.at[p], s_slpr.at[p]).wait()
+    for p in both:
+        afwd(p, 4)
+        afwd(p, 6)
+    for p in both:
+        ywait(p, 3)
+        ysend(p, 3, -1)
+        ywait(p, 7)
+        ysend(p, 7, 1)
+    for p in both:
+        arrived(slp.at[p], s_slpr.at[p])
 
     def pack(p, g, k):
         n = g * 4 + k
-        if k > 0:
-            pltpu.make_async_copy(
-                raw.at[p, k, pl.ds(4 * g, 4)], raw.at[p, k, pl.ds(4 * g, 4)], s_ar.at[p, k, g]
-            ).wait()
+        if k == 2:
+            arrived(raw.at[p, 2, 4 * g:4 * g + 4, 0:ZF], s_ar.at[p, 2, g])
         key = keys[p][:, 0:1]
         picks = []
         for w in range(4):
@@ -217,10 +270,22 @@
                         device_id=bdev(p, far, dc), device_id_type=MESH,
                     ).start()
 
-    for g in range(2):
-        for k in (0, 1, 3, 2):
-            for p in range(2):
-                pack(p, g, k)
+    for k in (0, 1, 3):
+        for p in both:
+            pack(p, 0, k)
+    for p in both:
+        ywait(p, 4)
+        ywait(p, 6)
+        ysend(p, 4, -1) if p == 0 else ysend(p, 6, 1)
+    for p in both:
+        pack(p, 0, 2)
+    for p in both:
+        afwd(p, 5)
+    for p in both:
+        ywait(p, 5)
+    for k in (0, 1, 3, 2):
+        for p in both:
+            pack(p, 1, k)
 
     ce_copy.wait()
     for p in range(2):
@@ -260,15 +325,9 @@
             stt[8 * q + v, 1:2, :] = totals[v:v + 1, :]
     rs[my_u] = stt[my_u]
 
-    def send_stats(t, carry):
+    for t in range(1, 32):
         dev, u = plane(t)
-        pltpu.make_async_remote_copy(
-            src_ref=stt.at[u], dst_ref=rs.at[my_u], send_sem=s_sts, recv_sem=s_str,
-            device_id=dev, device_id_type=MESH,
-        ).start()
-        return carry
-
-    lax.fori_loop(1, 32, send_stats, 0)
+        send(stt.at[u], rs.at[my_u], s_sts, s_str, dev)
     pltpu.make_async_copy(rs.at[0:31], rs.at[0:31], s_str).wait()
 
     m_in = jnp.concatenate([rs[d, 0:1, :] for d in range(32)], axis=0)
@@ -325,15 +384,9 @@
         lt[d, 0:1, :] = back[d:d + 1, :]
     lr[my_u] = lt[my_u]
 
-    def send_norm(t, carry):
+    for t in range(1, 32):
         dev, u = plane(t)
-        pltpu.make_async_remote_copy(
-            src_ref=lt.at[u], dst_ref=lr.at[my_u], send_sem=s_ls, recv_sem=s_lr,
-            device_id=dev, device_id_type=MESH,
-        ).start()
-        return carry
-
-    lax.fori_loop(1, 32, send_norm, 0)
+        send(lt.at[u], lr.at[my_u], s_ls, s_lr, dev)
 
     slot_i = slz[1, 0:1, :].astype(jnp.int32)
     lane_of = ((slot_i // 4) % 4) * 32 + 4 + slot_i % 4
@@ -373,26 +426,25 @@
         for i, col in ((1, far_col), (0, own_col)):
             sums = jnp.dot(wb[...], inc[j, :, pl.ds(col, HALF)], preferred_element_type=F32)
             prev = ce[rows, pl.ds(col, HALF)].astype(F32)
-            fr[i, rows, :] = (sums + LAMBDA * prev) / denom
+            fresh = (sums + LAMBDA * prev) / denom
             if i == 1:
-                pltpu.make_async_remote_copy(
-                    src_ref=fr.at[1, rows], dst_ref=out.at[at], send_sem=s_fs, recv_sem=s_fr,
-                    device_id=(dp, 1 - c), device_id_type=MESH,
-                ).start()
+                fr[rows, :] = fresh
+                send(fr.at[rows], out.at[at], s_fs, s_fr, (dp, 1 - c))
             else:
-                pltpu.make_async_copy(fr.at[0, rows], out.at[at], s_fl).start()
+                out[at, :] = fresh
         return carry
 
     lax.fori_loop(0, OWN, update, 0)
 
-    pltpu.make_async_copy(fr.at[0], fr.at[0], s_fl).wait()
-    pltpu.make_async_copy(fr.at[1], fr.at[1], s_fs).wait()
-    pltpu.make_async_copy(fr.at[1], fr.at[1], s_fr).wait()
-    for p in range(2):
-        pltpu.make_async_copy(raw.at[p, 0, 0:7], raw.at[p, 0, 0:7], s_zs.at[p]).wait()
-        pltpu.make_async_copy(raw.at[p, 1:4], raw.at[p, 1:4], s_as.at[p]).wait()
-        pltpu.make_async_copy(slp.at[p], slp.at[p], s_slps.at[p]).wait()
-        pltpu.make_async_copy(pk.at[p, :, 1:8], pk.at[p, :, 1:8], s_ps.at[p]).wait()
+    arrived(fr, s_fs)
+    arrived(fr, s_fr)
+    for p in both:
+        arrived(raw.at[p, 0, 0:7, 0:ZF], s_zs.at[p])
+        arrived(raw.at[p, 1:4, :, 0:ZF], s_as.at[p])
+        arrived(raw.at[p, 1:4, 1, ZF:ROWS], s_bs.at[p])
+        arrived(raw.at[p, :, 0:7, ZF:ROWS], s_ys.at[p])
+        arrived(slp.at[p], s_slps.at[p])
+        arrived(pk.at[p, :, 1:8], s_ps.at[p])
     pltpu.make_async_copy(slz.at[0:7], slz.at[0:7], s_slzs).wait()
     pltpu.make_async_copy(stt.at[0:31], stt.at[0:31], s_sts).wait()
     pltpu.make_async_copy(tz.at[1:8], tz.at[1:8], s_tzs).wait()
@@ -413,7 +465,7 @@
             pl.BlockSpec(memory_space=vmem),
             pl.BlockSpec(memory_space=pl.ANY),
         ],
-        out_specs=(pl.BlockSpec(memory_space=pl.ANY), pl.BlockSpec(memory_space=vmem)),
+        out_specs=(pl.BlockSpec(memory_space=vmem), pl.BlockSpec(memory_space=vmem)),
         scratch_shapes=[
             vmem((2, 4, 8, ROWS, HALF), BF16),
             vmem((8, 24, 128), F32),
@@ -430,15 +482,16 @@
             vmem((32, 8, 128), F32),
             vmem((32, 8, 128), F32),
             vmem((BS, 1024), BF16),
-            vmem((2, OWN * BS, HALF), F32),
+            vmem((OWN * BS, HALF), F32),
             vmem((2, 512, 128), F32),
             vmem((128, 128), F32),
-            dma((2,)), dma((2, 8)), dma((2,)), dma((2, 4, 2)),
+            dma((2,)), dma((2, 8)), dma((2,)), dma((2, 4, 8)),
+            dma((2,)), dma((2,)), dma((2,)), dma((2, 8)),
             dma, dma, dma((2,)), dma((2,)), dma((2,)), dma((2,)), dma((2,)), dma,
-            dma, dma, dma, dma, dma, dma, dma, dma, dma,
+            dma, dma, dma, dma, dma, dma, dma, dma,
         ],
         compiler_params=pltpu.CompilerParams(
-            collective_id=0, has_side_effects=True, vmem_limit_bytes=56 * 1024 * 1024
+            collective_id=0, has_side_effects=True, vmem_limit_bytes=48 * 1024 * 1024
         ),
         cost_estimate=pl.CostEstimate(
             flops=8_000_000_000, bytes_accessed=10_000_000, transcendentals=1_000_000
@@ -446,8 +499,8 @@
         name="kmeans_step",
     )(
         embeddings,
-        parents.astype(F32).reshape(1, ROWS),
-        block_lists.reshape(8, 128),
+        parents.reshape(1, ROWS),
+        block_lists.T,
         centroids,
     )
     return fresh, spread.reshape(ROWS)

time: 143 us -> 126 us (0.88)
  Pallas kernels: 135 us -> 121 us
  local copies, waits for them, and re-layouts: 6.61 us -> 4.82 us
    pallas_call x1, Pallas kernels: 135 us -> 121 us  [local(): pl.pallas_call(kernel, out_shape=(jax.ShapeDtypeStruct((2 * OWN * BS, HAL...]
    unnamed x5 -> x8, local copies, waits for them, and re-layouts: 5.93 us -> 4.82 us
where the time goes in v2:
time: 126 us
  Pallas kernels  121 us (96%)
  local copies, waits for them, and re-layouts  4.82 us (4%)
    pallas_call x1, Pallas kernels, local(): pl.pallas_call(kernel, out_shape=(jax.ShapeDtypeStruct((2 * OWN * BS, HAL...  121 us
    unnamed x8, local copies, waits for them, and re-layouts  4.82 us

profile of v2, /device:TPU:1, one launch (start us, length us, event | category | flops | bytes accessed | tf_op | source)
XLA Modules:
  0.0 126.0 jit_solution(3624819637674433850)
XLA Ops:
  0.6 0.0 copy-start
  0.6 0.9 copy-done
  1.6 0.0 copy-start.1
  1.6 0.7 copy-done.1
  2.3 0.0 copy-start.2
  2.3 0.7 copy-done.2
  2.9 120.5 %kmeans_step.1 = (f32[2048,512]{1,0:T(8,128)S(1)}, f32[1,128]{1,0:T(1,128)S(1)}) custom-call(bf16[128,1024]{1,0:T(8,128)(2,1)S(1)} %copy-done, s32[1,128]{1,0:T(1,128)S(1)} %bitcast.4, s32[16,64]{1,0:T(8,128)S(1)} %bitcast.3, bf16[2048,1024]{1,0:T(8,128)(2,1)} %cent.1), custom_call_target="tpu_custom_call" | custom-call | flops 8000000000 | bytes 10000000 | tf_op jit(solution)/shard_map/kmeans_step/pallas_call | solution.py:456
  123.5 2.0 %copy.8 = f32[2048,512]{1,0:T(8,128)} copy(f32[2048,512]{1,0:T(8,128)S(1)} %get-tuple-element.8) | data formatting | bytes 8388608
  125.5 0.5 copy.9
Async XLA Ops:
  0.6 1.0 copy-start
  1.6 0.7 copy-start.1
  2.3 0.7 copy-start.2

commit v3 on v2

v3 whole, which is shorter than its diff:
```python
import math

import jax
import jax.numpy as jnp
from jax import lax
from jax.experimental import pallas as pl
from jax.experimental.pallas import tpu as pltpu
from jax.sharding import PartitionSpec as P

BETA = 3.0
LAMBDA = 0.25
EMPTY_NORM = 1e30
NONE_MAX = -1e30
MESH = pl.DeviceIdType.MESH

NY, NX, NZ, NC = 4, 4, 8, 2
ROWS = 128
D = 1024
HALF = 512
BS = 256
OWN = 4
CAP = 4
ZF = 64
ORDER = (1, 2, 0, 3, 7, 4, 6, 5)
F32 = jnp.float32
BF16 = jnp.bfloat16


def kernel(
    emb, par_in, bl_in, cent, out, spread,
    raw, slz, slp, pk, inc, ce, e_sc, ms, ss, stt, rs, tz, lt, lr, wb, fr, keys, pbq, par, bl,
    s_in, s_zs, s_zr, s_as, s_ar, s_bs, s_br, s_ys, s_yr, s_slzs, s_slzr, s_slps, s_slpr,
    s_ps, s_pr, s_loc, s_ce, s_sts, s_str, s_tzs, s_tzr, s_ls, s_lr, s_fs, s_fr,
):
    dp = lax.axis_index("dp")
    c = lax.axis_index("rep")
    y = dp // 32
    x = (dp // 8) % 4
    z = dp % 8
    first = c == 0
    a_me = jnp.where(first, y, x)
    b_me = jnp.where(first, x, y)
    a_unit = jnp.where(first, 32, 8)
    b_unit = jnp.where(first, 8, 32)

    def zdev(dz):
        return (dp - z + (z + dz) % 8, c)

    def adev(k):
        return (dp + ((a_me + k) % 4 - a_me) * a_unit, c)

    def bdev(k, dc):
        return (dp + ((b_me + k) % 4 - b_me) * b_unit, c if dc == 0 else 1 - c)

    ys = [(y + t) % 4 for t in range(4)]
    xs = [(x + t) % 4 for t in range(4)]

    def plane(t):
        yy, xx = ys[t // 8], xs[(t // 2) % 4]
        cc = c if t % 2 == 0 else 1 - c
        u = jnp.where(cc == 0, xx * 4 + yy, 16 + yy * 4 + xx)
        return ((yy * 4 + xx) * 8 + z, cc), u

    my_u = c * 16 + b_me * 4 + a_me

    def send(src, dst, ssem, rsem, dev):
        pltpu.make_async_remote_copy(
            src_ref=src, dst_ref=dst, send_sem=ssem, recv_sem=rsem,
            device_id=dev, device_id_type=MESH,
        ).start()

    def arrived(ref, sem):
        pltpu.make_async_copy(ref, ref, sem).wait()

    emb_copy = pltpu.make_async_copy(emb, raw.at[1, 0], s_in.at[0])
    par_copy = pltpu.make_async_copy(par_in, par, s_in.at[1])
    bl_copy = pltpu.make_async_copy(bl_in, bl, s_in.at[2])
    ce_copy = pltpu.make_async_copy(cent.at[pl.ds(c * 1024, 1024)], ce, s_ce)
    emb_copy.start()
    par_copy.start()
    bl_copy.start()
    ce_copy.start()

    barrier = pltpu.get_barrier_semaphore()
    for t in range(1, 32):
        pl.semaphore_signal(barrier, 1, device_id=plane(t)[0], device_id_type=MESH)
    for dz in range(1, 8):
        pl.semaphore_signal(barrier, 1, device_id=zdev(dz), device_id_type=MESH)
    emb_copy.wait()
    pl.semaphore_wait(barrier, 38)

    def step_to(pos, step):
        return (pos + 1) % 8 if step < 0 else (pos - 1) % 8

    def zsend(pos, step, lo=0, hi=D):
        to = step_to(pos, step)
        send(
            raw.at[pos, 0, 0:ZF, lo:hi], raw.at[to, 0, 0:ZF, lo:hi],
            s_zs, s_zr.at[to], zdev(step),
        )

    def zwait(pos):
        arrived(raw.at[pos, 0, 0:ZF], s_zr.at[pos])

    def asend(pos):
        for k in (1, 3):
            send(raw.at[pos, 0, 0:ZF], raw.at[pos, 4 - k, 0:ZF], s_as, s_ar.at[4 - k, pos], adev(k))

    def afwd(pos):
        for k, lo, hi in ((1, 0, HALF), (3, HALF, D)):
            arrived(raw.at[pos, k, 0:ZF], s_ar.at[k, pos])
            send(
                raw.at[pos, k, 0:ZF, lo:hi], raw.at[pos, 2, 0:ZF, lo:hi],
                s_as, s_ar.at[2, pos], adev(4 - k),
            )

    def bsend():
        for k in (1, 3, 2):
            send(raw.at[1, 0, ZF:ROWS], raw.at[1, 4 - k, ZF:ROWS], s_bs, s_br, adev(k))

    def bwait():
        arrived(raw.at[1, 1:4, ZF:ROWS], s_br)

    def ysend(pos, step, lo=0, hi=D):
        to = step_to(pos, step)
        send(
            raw.at[pos, :, ZF:ROWS, lo:hi], raw.at[to, :, ZF:ROWS, lo:hi],
            s_ys, s_yr.at[to], zdev(step),
        )

    def ywait(pos):
        arrived(raw.at[pos, :, ZF:ROWS], s_yr.at[pos])

    def pack(pos):
        tau = ORDER.index(pos)
        arrived(raw.at[pos, 2, 0:ZF], s_ar.at[2, pos])
        key = keys[:, 0:1]
        picks = []
        for k in range(4):
            s_row = slz[pos, 0:1, :] if k == 0 else slp[k - 1, pos, 0:1, :]
            picks.append(jnp.where(key == s_row + float(256 * k), 1.0, 0.0).astype(BF16))
        pick = jnp.concatenate(picks, axis=1)
        rows = raw[pos].reshape(512, D)
        packed = jnp.dot(pick, rows, preferred_element_type=F32).astype(BF16)
        pk[tau] = packed.reshape(8, OWN, 16, D)
        off = pl.multiple_of(tau * 128 + c * 64 + b_me * 16, 16)
        dst = inc.at[:, pl.ds(off, 16), :]
        for far in (1, 3, 2, 0):
            for dc in range(2):
                i = far * 2 + dc
                if i == 0:
                    pltpu.make_async_copy(pk.at[tau, 0], dst, s_loc.at[tau]).start()
                else:
                    send(pk.at[tau, i], dst, s_ps, s_pr.at[tau], bdev(far, dc))

    zsend(1, -1)
    zsend(1, 1)
    asend(1)
    bsend()
    zwait(2)
    zsend(2, -1)
    zwait(0)
    zsend(0, 1)
    asend(2)
    afwd(1)
    asend(0)

    par_copy.wait()
    bl_copy.wait()
    par_row = par[0:1, :].astype(F32)
    sub = lax.broadcasted_iota(jnp.int32, (ROWS, ROWS), 0)
    lane = lax.broadcasted_iota(jnp.int32, (ROWS, ROWS), 1)
    par_wide = jnp.broadcast_to(par_row, (ROWS, ROWS))
    par_col = jnp.sum(jnp.where(sub == lane, par_wide, 0.0), axis=1, keepdims=True)
    earlier = jnp.where((par_col == par_wide) & (sub < lane), 1.0, 0.0)
    slot_row = par_row * CAP + jnp.sum(earlier, axis=0, keepdims=True)
    slot_col = jnp.sum(
        jnp.where(sub == lane, jnp.broadcast_to(slot_row, (ROWS, ROWS)), 0.0), axis=1, keepdims=True
    )
    slz[1, 0:8, :] = jnp.broadcast_to(slot_row, (8, 128))
    code = ((lane // 32) * CAP + lane % CAP).astype(F32)
    for p4 in range(16):
        hit = jnp.where(slot_col == code + float(16 * p4), 1.0, 0.0)
        slz[1, 8 + p4:9 + p4, :] = jnp.sum(hit, axis=0, keepdims=True)
    for dz in range(1, 8):
        send(slz.at[1], slz.at[(1 - dz) % 8], s_slzs, s_slzr, zdev(dz))

    bwait()
    zwait(3)
    zsend(3, -1)
    zwait(7)
    zsend(7, 1)
    asend(3)
    arrived(slz.at[0:7], s_slzr)
    for k in (1, 3, 2):
        send(slz.at[:, 0:8, :], slp.at[3 - k], s_slps, s_slpr, adev(k))
    afwd(2)
    ysend(1, -1)
    ysend(1, 1)
    asend(7)

    lists = jnp.concatenate([bl[0:8, :], bl[8:16, :]], axis=1)
    which = (lax.broadcasted_iota(jnp.int32, (1, 128), 1) % 64).astype(F32)

    def lookup(ids):
        acc = jnp.zeros((ids.shape[0], 128), F32)
        for ch in range(8):
            acc += jnp.where(ids == lists[ch:ch + 1, :], which, 0.0)
        return jnp.sum(acc, axis=1, keepdims=True)

    row = lax.broadcasted_iota(jnp.int32, (512, 1), 0)
    far_chip = dp + ((b_me + row // 128) % 4 - b_me) * b_unit
    core = jnp.where((row // 64) % 2 == 0, c, 1 - c)
    word = ((row // 4) % 4 + 4 - a_me) % 4
    keys[...] = jnp.broadcast_to(
        lookup(far_chip * 8 + core * 4 + (row // 16) % 4) * CAP
        + (row % 4).astype(F32) + (word * 256).astype(F32),
        (512, 128),
    )
    r128 = lax.broadcasted_iota(jnp.int32, (128, 1), 0)
    peer = r128 % 32
    high, low = (peer // 4) % 4, peer % 4
    peer_y = jnp.where(peer < 16, low, high)
    peer_x = jnp.where(peer < 16, high, low)
    peer_first = ((peer_y * 4 + peer_x) * 8 + z) * 8 + (peer // 16) * 4
    wide = jnp.zeros((128, 128), F32)
    for q in range(4):
        ids = peer_first + (q + 4 - r128 // 32) % 4
        wide = jnp.where(lane // 32 == q, lookup(ids) - float(q), wide)
    pbq[...] = wide

    zwait(4)
    zsend(4, -1, 0, HALF)
    zwait(6)
    zsend(6, 1, HALF, D)
    asend(6)
    afwd(0)
    asend(4)
    arrived(slp, s_slpr)
    pack(1)
    afwd(3)
    afwd(7)
    afwd(6)
    ywait(2)
    ysend(2, -1)
    ywait(0)
    ysend(0, 1)
    zwait(5)
    asend(5)
    afwd(4)
    pack(0)
    pack(2)
    ywait(3)
    ysend(3, -1)
    ywait(7)
    ysend(7, 1)
    pack(7)
    afwd(5)
    pack(3)
    ywait(4)
    ysend(4, -1, 0, HALF)
    ywait(6)
    ysend(6, 1, HALF, D)
    pack(6)
    pack(4)
    ywait(5)
    pack(5)

    ce_copy.wait()
    scale = BETA / math.sqrt(D)
    for n in range(4):
        for tau in (2 * n, 2 * n + 1):
            arrived(inc.at[:, tau * 128:tau * 128 + 112], s_pr.at[tau])
            arrived(inc.at[:, tau * 128:tau * 128 + 16], s_loc.at[tau])

        def score(j, carry, n=n):
            s = lax.dot_general(
                ce[pl.ds(pl.multiple_of(j * BS, BS), BS), :], inc[j, n * 256:(n + 1) * 256, :],
                (((1,), (1,)), ((), ())), preferred_element_type=F32,
            ) * scale
            top = jnp.max(s, axis=0, keepdims=True)
            e = jnp.exp(s - top)
            e_sc[j, n] = e
            total = jnp.sum(e, axis=0, keepdims=True)
            for h in range(2):
                ms[j, 2 * n + h:2 * n + h + 1, :] = top[:, h * 128:(h + 1) * 128]
                ss[j, 2 * n + h:2 * n + h + 1, :] = total[:, h * 128:(h + 1) * 128]
            return carry

        lax.fori_loop(0, OWN, score, 0)

    sub32 = lax.broadcasted_iota(jnp.int32, (32, 128), 0)
    lane32 = lax.broadcasted_iota(jnp.int32, (32, 128), 1)
    window = ((lane32 + 128 - 4 * sub32) % 128) // 4
    tops = jnp.zeros((32, 128), F32)
    totals = jnp.zeros((32, 128), F32)
    for j in range(OWN):
        for tau, pos in enumerate(ORDER):
            here = window == 8 * j + pos
            turn = 32 * j + 4 * pos
            m_row, s_row = ms[j, tau:tau + 1, :], ss[j, tau:tau + 1, :]
            if turn:
                m_row, s_row = pltpu.roll(m_row, turn, 1), pltpu.roll(s_row, turn, 1)
            tops = jnp.where(here, m_row, tops)
            totals = jnp.where(here, s_row, totals)
    for u in range(32):
        m_row, s_row = tops[u:u + 1, :], totals[u:u + 1, :]
        if u:
            m_row, s_row = pltpu.roll(m_row, 128 - 4 * u, 1), pltpu.roll(s_row, 128 - 4 * u, 1)
        stt[u, 0:1, :] = m_row
        stt[u, 1:2, :] = s_row
    rs[my_u] = stt[my_u]
    for t in range(1, 32):
        dev, u = plane(t)
        send(stt.at[u], rs.at[my_u], s_sts, s_str, dev)
    arrived(rs.at[0:31], s_str)

    m_in = jnp.concatenate([rs[d, 0:1, :] for d in range(32)], axis=0)
    s_in = jnp.concatenate([rs[d, 1:2, :] for d in range(32)], axis=0)
    m_all = jnp.concatenate([m_in] + [pltpu.roll(m_in, 32 * k, 1) for k in (1, 2, 3)], axis=0)
    s_all = jnp.concatenate([s_in] + [pltpu.roll(s_in, 32 * k, 1) for k in (1, 2, 3)], axis=0)
    owner = pbq[...]
    m_back = jnp.zeros((128, 128), F32)
    for p4 in range(16):
        mine = owner == float(4 * p4)
        top = jnp.max(jnp.where(mine, m_all, NONE_MAX), axis=0, keepdims=True)
        tz[0, 0, p4:p4 + 1, :] = top
        m_back = jnp.where(mine, top, m_back)
    z_all = s_all * jnp.exp(m_all - m_back)
    for p4 in range(16):
        mine = owner == float(4 * p4)
        tz[0, 1, p4:p4 + 1, :] = jnp.sum(jnp.where(mine, z_all, 0.0), axis=0, keepdims=True)

    for dz in range(1, 8):
        pltpu.make_async_remote_copy(
            src_ref=tz.at[0], dst_ref=tz.at[8 - dz], send_sem=s_tzs, recv_sem=s_tzr,
            device_id=zdev(dz), device_id_type=MESH,
        ).start()
    place = lax.broadcasted_iota(jnp.int32, (16, 128), 1) % 32
    filled = jnp.zeros((16, 128), F32)
    for pos in range(8):
        filled = jnp.where(place // 4 == pos, slz[pos, 8:24, :], filled)
    pltpu.make_async_copy(tz.at[1:8], tz.at[1:8], s_tzr).wait()

    def aligned(dz, what):
        t = tz[dz, what]
        if dz == 0:
            return t
        turn = 4 * dz
        return jnp.where(place >= turn, pltpu.roll(t, turn, 1), pltpu.roll(t, 96 + turn, 1))

    tops = [aligned(dz, 0) for dz in range(8)]
    highest = tops[0]
    for t in tops[1:]:
        highest = jnp.maximum(highest, t)
    summed = jnp.zeros((16, 128), F32)
    for dz in range(8):
        summed += aligned(dz, 1) * jnp.exp(tops[dz] - highest)
    log_total = jnp.log(summed)
    norm = jnp.where(filled > 0.5, highest + log_total, EMPTY_NORM)

    turned = jnp.zeros((128, 128), F32)
    for p4 in range(16):
        turned = jnp.where(owner == float(4 * p4), norm[p4:p4 + 1, :], turned)
    back = turned[0:32]
    for k in (1, 2, 3):
        back += pltpu.roll(turned[32 * k:32 * k + 32], 128 - 32 * k, 1)
    for d in range(32):
        lt[d, 0:1, :] = back[d:d + 1, :]
    lr[my_u] = lt[my_u]

    for t in range(1, 32):
        dev, u = plane(t)
        send(lt.at[u], lr.at[my_u], s_ls, s_lr, dev)

    slot_i = slz[1, 0:1, :].astype(jnp.int32)
    lane_of = ((slot_i // 4) % 4) * 32 + 4 + slot_i % 4
    choose = jnp.where(sub == jnp.broadcast_to(lane_of, (128, 128)), 1.0, 0.0)
    by_lane = jnp.dot(
        log_total, choose, preferred_element_type=F32, precision=lax.Precision.HIGHEST
    )
    p4_row = lax.broadcasted_iota(jnp.int32, (16, 128), 0)
    spread[0:1, :] = jnp.sum(
        jnp.where(p4_row == jnp.broadcast_to(slot_i // 16, (16, 128)), by_lane, 0.0),
        axis=0, keepdims=True,
    )

    pltpu.make_async_copy(lr.at[0:31], lr.at[0:31], s_lr).wait()

    turned = jnp.concatenate(
        [lr[u, 0:1, :] if u == 0 else pltpu.roll(lr[u, 0:1, :], 4 * u, 1) for u in range(32)], axis=0
    )
    for j in range(OWN):
        for tau, pos in enumerate(ORDER):
            got = jnp.where(window == 8 * j + pos, turned, 0.0)
            got = jnp.sum(got, axis=0, keepdims=True)
            turn = 32 * j + 4 * pos
            ss[j, tau:tau + 1, :] = pltpu.roll(got, 128 - turn, 1) if turn else got
    own_col = pl.multiple_of(c * HALF, HALF)
    far_col = pl.multiple_of((1 - c) * HALF, HALF)

    def update(j, carry):
        factor = jnp.exp(ms[j] - ss[j])
        mass = jnp.zeros((BS, 128), F32)
        for n in range(4):
            for h in range(2):
                v = 2 * n + h
                w = e_sc[j, n, :, h * 128:(h + 1) * 128] * factor[v:v + 1, :]
                mass += w
                wb[:, v * 128:(v + 1) * 128] = w.astype(BF16)
        denom = jnp.sum(mass, axis=1, keepdims=True) + LAMBDA
        rows = pl.ds(pl.multiple_of(j * BS, BS), BS)
        at = pl.ds(pl.multiple_of((c * OWN + j) * BS, BS), BS)
        for i, col in ((1, far_col), (0, own_col)):
            sums = jnp.dot(wb[...], inc[j, :, pl.ds(col, HALF)], preferred_element_type=F32)
            prev = ce[rows, pl.ds(col, HALF)].astype(F32)
            fresh = (sums + LAMBDA * prev) / denom
            if i == 1:
                fr[rows, :] = fresh
                send(fr.at[rows], out.at[at], s_fs, s_fr, (dp, 1 - c))
            else:
                out[at, :] = fresh
        return carry

    lax.fori_loop(0, OWN, update, 0)

    arrived(fr, s_fs)
    arrived(fr, s_fr)
    arrived(raw.at[0:7, 0, 0:ZF], s_zs)
    arrived(raw.at[:, 1:4, 0:ZF], s_as)
    arrived(raw.at[1, 1:4, ZF:ROWS], s_bs)
    arrived(raw.at[0:7, :, ZF:ROWS], s_ys)
    arrived(slz.at[0:7], s_slzs)
    arrived(slp, s_slps)
    arrived(pk.at[:, 1:8], s_ps)
    arrived(stt.at[0:31], s_sts)
    arrived(tz.at[1:8], s_tzs)
    arrived(lt.at[0:31], s_ls)


def local(embeddings, parents, block_lists, centroids):
    dma, vmem = pltpu.SemaphoreType.DMA, pltpu.VMEM
    fresh, spread = pl.pallas_call(
        kernel,
        out_shape=(
            jax.ShapeDtypeStruct((2 * OWN * BS, HALF), F32),
            jax.ShapeDtypeStruct((1, ROWS), F32),
        ),
        in_specs=[pl.BlockSpec(memory_space=pltpu.HBM)] * 4,
        out_specs=(pl.BlockSpec(memory_space=vmem), pl.BlockSpec(memory_space=vmem)),
        scratch_shapes=[
            vmem((8, 4, ROWS, D), BF16),
            vmem((8, 24, 128), F32),
            vmem((3, 8, 8, 128), F32),
            vmem((8, 8, OWN, 16, D), BF16),
            vmem((OWN, 1024, D), BF16),
            vmem((OWN * BS, D), BF16),
            vmem((OWN, 4, BS, 256), F32),
            vmem((OWN, 8, 128), F32),
            vmem((OWN, 8, 128), F32),
            vmem((32, 8, 128), F32),
            vmem((32, 8, 128), F32),
            vmem((8, 2, 16, 128), F32),
            vmem((32, 8, 128), F32),
            vmem((32, 8, 128), F32),
            vmem((BS, 1024), BF16),
            vmem((OWN * BS, HALF), F32),
            vmem((512, 128), F32),
            vmem((128, 128), F32),
            vmem((1, ROWS), jnp.int32),
            vmem((16, 64), jnp.int32),
            dma((3,)), dma, dma((8,)), dma, dma((4, 8)), dma, dma, dma, dma((8,)),
            dma, dma, dma, dma,
            dma, dma((8,)), dma((8,)), dma, dma, dma, dma, dma, dma, dma, dma, dma,
        ],
        compiler_params=pltpu.CompilerParams(
            collective_id=0, has_side_effects=True, vmem_limit_bytes=48 * 1024 * 1024
        ),
        cost_estimate=pl.CostEstimate(
            flops=8_000_000_000, bytes_accessed=10_000_000, transcendentals=1_000_000
        ),
        name="kmeans_step",
    )(
        embeddings,
        parents.reshape(1, ROWS),
        block_lists.T,
        centroids,
    )
    return fresh, spread.reshape(ROWS)


def solution(mesh):
    placed = (P(("dp", "rep"), None), P(("dp", "rep")), P(), P("dp", None))
    return jax.shard_map(
        local,
        mesh=mesh,
        in_specs=placed,
        out_specs=(P("dp", "rep"), P(("dp", "rep"))),
        check_vma=False,
    )
```

time: 126 us -> 115 us (0.913)
  Pallas kernels: 121 us -> 109 us
    pallas_call x1, Pallas kernels: 121 us -> 109 us  [local(): pl.pallas_call(kernel, out_shape=(jax.ShapeDtypeStruct((2 * OWN * BS, HAL...]
where the time goes in v3:
time: 115 us
  Pallas kernels  109 us (95%)
  local copies, waits for them, and re-layouts  4.82 us (4%)
    pallas_call x1, Pallas kernels, local(): pl.pallas_call(kernel, out_shape=(jax.ShapeDtypeStruct((2 * OWN * BS, HAL...  109 us
    unnamed x8, local copies, waits for them, and re-layouts  4.82 us

profile of v3, /device:TPU:1, one launch (start us, length us, event | category | flops | bytes accessed | tf_op | source)
XLA Modules:
  0.0 114.8 jit_solution(3885044058348876441)
XLA Ops:
  0.6 0.0 copy-start
  0.6 0.9 copy-done
  1.6 0.0 copy-start.1
  1.6 0.7 copy-done.1
  2.3 0.0 copy-start.2
  2.3 0.7 copy-done.2
  2.9 109.4 %kmeans_step.1 = (f32[2048,512]{1,0:T(8,128)S(1)}, f32[1,128]{1,0:T(1,128)S(1)}) custom-call(bf16[128,1024]{1,0:T(8,128)(2,1)S(1)} %copy-done, s32[1,128]{1,0:T(1,128)S(1)} %bitcast.4, s32[16,64]{1,0:T(8,128)S(1)} %bitcast.3, bf16[2048,1024]{1,0:T(8,128)(2,1)} %cent.1), custom_call_target="tpu_custom_call" | custom-call | flops 8000000000 | bytes 10000000 | tf_op jit(solution)/shard_map/kmeans_step/pallas_call | solution.py:443
  112.3 2.0 %copy.8 = f32[2048,512]{1,0:T(8,128)} copy(f32[2048,512]{1,0:T(8,128)S(1)} %get-tuple-element.8) | data formatting | bytes 8388608
  114.3 0.5 copy.9
Async XLA Ops:
  0.6 1.0 copy-start
  1.6 0.7 copy-start.1
  2.3 0.7 copy-start.2

commit v4 on v3

--- a/solution.py
+++ b/solution.py
@@ -22,13 +22,15 @@
 CAP = 4
 ZF = 64
 ORDER = (1, 2, 0, 3, 7, 4, 6, 5)
+PLANE = sorted(range(1, 32), key=lambda t: -(min(t // 8, 4 - t // 8) + min(t // 2 % 4, 4 - t // 2 % 4)))
+RING = (4, 3, 5, 2, 6, 1, 7)
 F32 = jnp.float32
 BF16 = jnp.bfloat16
 
 
 def kernel(
     emb, par_in, bl_in, cent, out, spread,
-    raw, slz, slp, pk, inc, ce, e_sc, ms, ss, stt, rs, tz, lt, lr, wb, fr, keys, pbq, par, bl,
+    raw, slz, slp, pk, inc, ce, e_sc, ms, ss, stt, rs, tz, lt, lr, wb, dn, fr, keys, pbq, par, bl,
     s_in, s_zs, s_zr, s_as, s_ar, s_bs, s_br, s_ys, s_yr, s_slzs, s_slzr, s_slps, s_slpr,
     s_ps, s_pr, s_loc, s_ce, s_sts, s_str, s_tzs, s_tzr, s_ls, s_lr, s_fs, s_fr,
 ):
@@ -82,9 +84,9 @@
     ce_copy.start()
 
     barrier = pltpu.get_barrier_semaphore()
-    for t in range(1, 32):
+    for t in PLANE:
         pl.semaphore_signal(barrier, 1, device_id=plane(t)[0], device_id_type=MESH)
-    for dz in range(1, 8):
+    for dz in RING:
         pl.semaphore_signal(barrier, 1, device_id=zdev(dz), device_id_type=MESH)
     emb_copy.wait()
     pl.semaphore_wait(barrier, 38)
@@ -182,7 +184,7 @@
     for p4 in range(16):
         hit = jnp.where(slot_col == code + float(16 * p4), 1.0, 0.0)
         slz[1, 8 + p4:9 + p4, :] = jnp.sum(hit, axis=0, keepdims=True)
-    for dz in range(1, 8):
+    for dz in RING:
         send(slz.at[1], slz.at[(1 - dz) % 8], s_slzs, s_slzr, zdev(dz))
 
     bwait()
@@ -310,7 +312,7 @@
         stt[u, 0:1, :] = m_row
         stt[u, 1:2, :] = s_row
     rs[my_u] = stt[my_u]
-    for t in range(1, 32):
+    for t in PLANE:
         dev, u = plane(t)
         send(stt.at[u], rs.at[my_u], s_sts, s_str, dev)
     arrived(rs.at[0:31], s_str)
@@ -331,7 +333,7 @@
         mine = owner == float(4 * p4)
         tz[0, 1, p4:p4 + 1, :] = jnp.sum(jnp.where(mine, z_all, 0.0), axis=0, keepdims=True)
 
-    for dz in range(1, 8):
+    for dz in RING:
         pltpu.make_async_remote_copy(
             src_ref=tz.at[0], dst_ref=tz.at[8 - dz], send_sem=s_tzs, recv_sem=s_tzr,
             device_id=zdev(dz), device_id_type=MESH,
@@ -369,7 +371,7 @@
         lt[d, 0:1, :] = back[d:d + 1, :]
     lr[my_u] = lt[my_u]
 
-    for t in range(1, 32):
+    for t in PLANE:
         dev, u = plane(t)
         send(lt.at[u], lr.at[my_u], s_ls, s_lr, dev)
 
@@ -407,22 +409,27 @@
                 v = 2 * n + h
                 w = e_sc[j, n, :, h * 128:(h + 1) * 128] * factor[v:v + 1, :]
                 mass += w
-                wb[:, v * 128:(v + 1) * 128] = w.astype(BF16)
+                wb[j, :, v * 128:(v + 1) * 128] = w.astype(BF16)
         denom = jnp.sum(mass, axis=1, keepdims=True) + LAMBDA
         rows = pl.ds(pl.multiple_of(j * BS, BS), BS)
+        dn[rows, :] = jnp.broadcast_to(denom, (BS, 128))
+        sums = jnp.dot(wb[j], inc[j, :, pl.ds(far_col, HALF)], preferred_element_type=F32)
+        prev = ce[rows, pl.ds(far_col, HALF)].astype(F32)
+        fr[rows, :] = (sums + LAMBDA * prev) / denom
         at = pl.ds(pl.multiple_of((c * OWN + j) * BS, BS), BS)
-        for i, col in ((1, far_col), (0, own_col)):
-            sums = jnp.dot(wb[...], inc[j, :, pl.ds(col, HALF)], preferred_element_type=F32)
-            prev = ce[rows, pl.ds(col, HALF)].astype(F32)
-            fresh = (sums + LAMBDA * prev) / denom
-            if i == 1:
-                fr[rows, :] = fresh
-                send(fr.at[rows], out.at[at], s_fs, s_fr, (dp, 1 - c))
-            else:
-                out[at, :] = fresh
+        send(fr.at[rows], out.at[at], s_fs, s_fr, (dp, 1 - c))
         return carry
 
+    def update_own(j, carry):
+        rows = pl.ds(pl.multiple_of(j * BS, BS), BS)
+        at = pl.ds(pl.multiple_of((c * OWN + j) * BS, BS), BS)
+        sums = jnp.dot(wb[j], inc[j, :, pl.ds(own_col, HALF)], preferred_element_type=F32)
+        prev = ce[rows, pl.ds(own_col, HALF)].astype(F32)
+        out[at, :] = (sums + LAMBDA * prev) / dn[rows, 0:1]
+        return carry
+
     lax.fori_loop(0, OWN, update, 0)
+    lax.fori_loop(0, OWN, update_own, 0)
 
     arrived(fr, s_fs)
     arrived(fr, s_fr)
@@ -463,7 +470,8 @@
             vmem((8, 2, 16, 128), F32),
             vmem((32, 8, 128), F32),
             vmem((32, 8, 128), F32),
-            vmem((BS, 1024), BF16),
+            vmem((OWN, BS, 1024), BF16),
+            vmem((OWN * BS, 128), F32),
             vmem((OWN * BS, HALF), F32),
             vmem((512, 128), F32),
             vmem((128, 128), F32),

time: 115 us -> 113 us (0.983)
  Pallas kernels: 109 us -> 107 us
    pallas_call x1, Pallas kernels: 109 us -> 107 us  [local(): pl.pallas_call(kernel, out_shape=(jax.ShapeDtypeStruct((2 * OWN * BS, HAL...]
where the time goes in v4:
time: 113 us
  Pallas kernels  107 us (95%)
  local copies, waits for them, and re-layouts  4.82 us (4%)
    pallas_call x1, Pallas kernels, local(): pl.pallas_call(kernel, out_shape=(jax.ShapeDtypeStruct((2 * OWN * BS, HAL...  107 us
    unnamed x8, local copies, waits for them, and re-layouts  4.82 us

profile of v4, /device:TPU:1, one launch (start us, length us, event | category | flops | bytes accessed | tf_op | source)
XLA Modules:
  0.0 112.5 jit_solution(5977990879516900535)
XLA Ops:
  0.6 0.0 copy-start
  0.6 0.9 copy-done
  1.6 0.0 copy-start.1
  1.6 0.7 copy-done.1
  2.3 0.0 copy-start.2
  2.3 0.7 copy-done.2
  2.9 107.0 %kmeans_step.1 = (f32[2048,512]{1,0:T(8,128)S(1)}, f32[1,128]{1,0:T(1,128)S(1)}) custom-call(bf16[128,1024]{1,0:T(8,128)(2,1)S(1)} %copy-done, s32[1,128]{1,0:T(1,128)S(1)} %bitcast.4, s32[16,64]{1,0:T(8,128)S(1)} %bitcast.3, bf16[2048,1024]{1,0:T(8,128)(2,1)} %cent.1), custom_call_target="tpu_custom_call" | custom-call | flops 8000000000 | bytes 10000000 | tf_op jit(solution)/shard_map/kmeans_step/pallas_call | solution.py:450
  110.0 2.0 %copy.8 = f32[2048,512]{1,0:T(8,128)} copy(f32[2048,512]{1,0:T(8,128)S(1)} %get-tuple-element.8) | data formatting | bytes 8388608
  112.0 0.5 copy.9
Async XLA Ops:
  0.6 1.0 copy-start
  1.6 0.7 copy-start.1
  2.3 0.7 copy-start.2

commit v5 on v4

--- a/solution.py
+++ b/solution.py
@@ -270,41 +270,42 @@
 
     ce_copy.wait()
     scale = BETA / math.sqrt(D)
-    for n in range(4):
-        for tau in (2 * n, 2 * n + 1):
-            arrived(inc.at[:, tau * 128:tau * 128 + 112], s_pr.at[tau])
-            arrived(inc.at[:, tau * 128:tau * 128 + 16], s_loc.at[tau])
-
-        def score(j, carry, n=n):
-            s = lax.dot_general(
-                ce[pl.ds(pl.multiple_of(j * BS, BS), BS), :], inc[j, n * 256:(n + 1) * 256, :],
-                (((1,), (1,)), ((), ())), preferred_element_type=F32,
-            ) * scale
-            top = jnp.max(s, axis=0, keepdims=True)
-            e = jnp.exp(s - top)
-            e_sc[j, n] = e
-            total = jnp.sum(e, axis=0, keepdims=True)
-            for h in range(2):
-                ms[j, 2 * n + h:2 * n + h + 1, :] = top[:, h * 128:(h + 1) * 128]
-                ss[j, 2 * n + h:2 * n + h + 1, :] = total[:, h * 128:(h + 1) * 128]
-            return carry
-
-        lax.fori_loop(0, OWN, score, 0)
-
     sub32 = lax.broadcasted_iota(jnp.int32, (32, 128), 0)
     lane32 = lax.broadcasted_iota(jnp.int32, (32, 128), 1)
     window = ((lane32 + 128 - 4 * sub32) % 128) // 4
     tops = jnp.zeros((32, 128), F32)
     totals = jnp.zeros((32, 128), F32)
-    for j in range(OWN):
-        for tau, pos in enumerate(ORDER):
-            here = window == 8 * j + pos
-            turn = 32 * j + 4 * pos
-            m_row, s_row = ms[j, tau:tau + 1, :], ss[j, tau:tau + 1, :]
-            if turn:
-                m_row, s_row = pltpu.roll(m_row, turn, 1), pltpu.roll(s_row, turn, 1)
-            tops = jnp.where(here, m_row, tops)
-            totals = jnp.where(here, s_row, totals)
+    for taus in ((0, 1), (2, 3), (4, 5), (6,), (7,)):
+        for tau in taus:
+            arrived(inc.at[:, tau * 128:tau * 128 + 112], s_pr.at[tau])
+            arrived(inc.at[:, tau * 128:tau * 128 + 16], s_loc.at[tau])
+
+        def score(j, carry, taus=taus):
+            lo, width = taus[0] * 128, len(taus) * 128
+            s = lax.dot_general(
+                ce[pl.ds(pl.multiple_of(j * BS, BS), BS), :], inc[j, lo:lo + width, :],
+                (((1,), (1,)), ((), ())), preferred_element_type=F32,
+            ) * scale
+            top = jnp.max(s, axis=0, keepdims=True)
+            e = jnp.exp(s - top)
+            e_sc[j, lo // 256, :, lo % 256:lo % 256 + width] = e
+            total = jnp.sum(e, axis=0, keepdims=True)
+            for h, tau in enumerate(taus):
+                ms[j, tau:tau + 1, :] = top[:, h * 128:(h + 1) * 128]
+                ss[j, tau:tau + 1, :] = total[:, h * 128:(h + 1) * 128]
+            return carry
+
+        lax.fori_loop(0, OWN, score, 0)
+        for j in range(OWN):
+            for tau in taus:
+                here = window == 8 * j + ORDER[tau]
+                turn = 32 * j + 4 * ORDER[tau]
+                m_row, s_row = ms[j, tau:tau + 1, :], ss[j, tau:tau + 1, :]
+                if turn:
+                    m_row, s_row = pltpu.roll(m_row, turn, 1), pltpu.roll(s_row, turn, 1)
+                tops = jnp.where(here, m_row, tops)
+                totals = jnp.where(here, s_row, totals)
+
     for u in range(32):
         m_row, s_row = tops[u:u + 1, :], totals[u:u + 1, :]
         if u:

time: 113 us -> 112 us (level)
  no operation moved by 1% of the time
where the time goes in v5:
time: 112 us
  Pallas kernels  107 us (96%)
  local copies, waits for them, and re-layouts  4.82 us (4%)
    pallas_call x1, Pallas kernels, local(): pl.pallas_call(kernel, out_shape=(jax.ShapeDtypeStruct((2 * OWN * BS, HAL...  107 us
    unnamed x8, local copies, waits for them, and re-layouts  4.82 us

profile of v5, /device:TPU:1, one launch (start us, length us, event | category | flops | bytes accessed | tf_op | source)
XLA Modules:
  0.0 112.2 jit_solution(17145648177187415358)
XLA Ops:
  0.6 0.0 copy-start
  0.6 0.9 copy-done
  1.6 0.0 copy-start.1
  1.6 0.7 copy-done.1
  2.3 0.0 copy-start.2
  2.3 0.7 copy-done.2
  2.9 106.7 %kmeans_step.1 = (f32[2048,512]{1,0:T(8,128)S(1)}, f32[1,128]{1,0:T(1,128)S(1)}) custom-call(bf16[128,1024]{1,0:T(8,128)(2,1)S(1)} %copy-done, s32[1,128]{1,0:T(1,128)S(1)} %bitcast.4, s32[16,64]{1,0:T(8,128)S(1)} %bitcast.3, bf16[2048,1024]{1,0:T(8,128)(2,1)} %cent.1), custom_call_target="tpu_custom_call" | custom-call | flops 8000000000 | bytes 10000000 | tf_op jit(solution)/shard_map/kmeans_step/pallas_call | solution.py:451
  109.7 2.0 %copy.8 = f32[2048,512]{1,0:T(8,128)} copy(f32[2048,512]{1,0:T(8,128)S(1)} %get-tuple-element.8) | data formatting | bytes 8388608
  111.7 0.5 copy.9
Async XLA Ops:
  0.6 1.0 copy-start
  1.6 0.7 copy-start.1
  2.3 0.7 copy-start.2
